TPU v7x, 32 devices: a whole 2x2x4 slice. The times are simulated.
32 devices in a mesh: groups: 2 (over y), fsdp: 4 (over z), rows: 2 (over x), tp: 2 (over core).
Axes of the slice: x: 2, y: 2, z: 4, core: 2. Of those that a mesh axis runs over, the one named last changes fastest.
Arguments:
- tokens: bfloat16 [768, 4, 8192], P(('groups', 'fsdp', 'rows'), None, 'tp'), parts along dimension 0, may hold values from -6 to 6
- queries: bfloat16 [768, 4, 32, 128], P(('groups', 'fsdp', 'rows'), None, 'tp'), parts along dimension 0, may hold values from -7 to 7
- kv_cache: bfloat16 [768, 32, 8, 256], P(('groups', 'fsdp', 'rows'), None, 'tp'), parts along dimension 0, may hold values from -6 to 6
- kv_weight: bfloat16 [8192, 8, 256], P('fsdp', 'tp'), may hold values from -0.0625 to 0.0625
- adapter_a: bfloat16 [128, 32, 8192], P(('fsdp', 'rows'), None, 'tp'), may hold values from -0.0625 to 0.0625
- adapter_b: bfloat16 [128, 2, 16, 8, 128], P(('fsdp', 'rows'), None, None, 'tp'), may hold values from -1.5 to 1.5
- adapter_id: int32 [768], P(('groups', 'fsdp', 'rows')), parts along dimension 0, may hold values from 0 to 127, as said below
- kv_len: int32 [768], P(('groups', 'fsdp', 'rows')), parts along dimension 0, may hold values from 2 to 32, as said below
Outputs:
- attended: bfloat16 [768, 4, 32, 128], P(('groups', 'fsdp', 'rows'), None, 'tp'), parts along dimension 0
- new_kv: bfloat16 [768, 4, 8, 256], P(('groups', 'fsdp', 'rows'), None, 'tp'), parts along dimension 0
There are 2 independent parts, one for each index of `groups`. A program takes and returns all parts, laid end to end along the dimension named above; an argument that names none is the same for every part. Nothing has to cross between parts.
Inputs may be any that keep to these rules, and one draw needn't show every extreme that they name: `adapter_id`: adapter a is owned by index a // 16 of fsdp and rows taken together. The rows of one device name adapters of exactly 4 owners, 12 rows for each. `kv_len`: each device has a row of length 32.
All inputs are finite; a program needn't handle non-finite values.
Results may differ from a plain program's by a relative error of at most 0.0055.
Values may be sent and summed in bfloat16 or wider, within the bound.
A program may use at most 128 MiB of HBM per device.

v0:
```python
import math

import jax
import jax.numpy as jnp
from jax import lax
from jax.sharding import PartitionSpec as P

ADP_DEV = 16


low_rank_scale = 0.5
rope_base = 500000.0


def rotate_keys(summed, positions):
    depth = summed.shape[-1] // 2
    half = depth // 2
    index = jnp.arange(half, dtype=jnp.int32).astype(jnp.float32)
    inverse = jnp.exp(index * (-2.0 * math.log(rope_base) / depth))
    angle = positions[..., None] * inverse
    cosine = jnp.cos(angle)[:, :, None, :]
    sine = jnp.sin(angle)[:, :, None, :]
    first = summed[..., :half]
    second = summed[..., half:depth]
    return jnp.concatenate(
        [first * cosine - second * sine, second * cosine + first * sine, summed[..., depth:]],
        axis=-1,
    )


def attend(queries, cache, fresh, lengths):
    batch, decode_steps, query_heads, depth = queries.shape
    kv_heads = cache.shape[2]
    context = cache.shape[1]
    grouped = queries.reshape(batch, decode_steps, kv_heads, query_heads // kv_heads, depth)
    scale = 1.0 / math.sqrt(depth)
    older = (
        jnp.einsum(
            "rsgqd,rpgd->rsgqp", grouped, cache[..., :depth], preferred_element_type=jnp.float32
        )
        * scale
    )
    newer = (
        jnp.einsum(
            "rsgqd,rtgd->rsgqt", grouped, fresh[..., :depth], preferred_element_type=jnp.float32
        )
        * scale
    )
    visible_old = jnp.arange(context, dtype=jnp.int32)[None, :] < lengths[:, None]
    visible_new = (
        jnp.arange(decode_steps, dtype=jnp.int32)[None, :]
        <= jnp.arange(decode_steps, dtype=jnp.int32)[:, None]
    )
    older = jnp.where(visible_old[:, None, None, None, :], older, -jnp.inf)
    newer = jnp.where(visible_new[None, :, None, None, :], newer, -jnp.inf)
    scores = jnp.concatenate([older, newer], axis=-1)
    top = jnp.max(scores, axis=-1, keepdims=True)
    weights = jnp.exp(scores - top)
    weights = (weights / jnp.sum(weights, axis=-1, keepdims=True)).astype(jnp.bfloat16)
    mixed = jnp.einsum(
        "rsgqp,rpgd->rsgqd",
        weights[..., :context],
        cache[..., depth:],
        preferred_element_type=jnp.float32,
    )
    mixed = mixed + jnp.einsum(
        "rsgqt,rtgd->rsgqd",
        weights[..., context:],
        fresh[..., depth:],
        preferred_element_type=jnp.float32,
    )
    return mixed.reshape(batch, decode_steps, query_heads, depth).astype(jnp.bfloat16)


def local(tokens, queries, kv_cache, kv_weight, adapter_a, adapter_b, adapter_id, kv_len):
    rows_dev, decode_steps, half_width = tokens.shape
    heads_per_shard = kv_weight.shape[1]
    rotary_pair_width = kv_weight.shape[2]
    rank_size = adapter_b.shape[2]
    owners = lax.axis_size(("fsdp", "rows"))
    capacity = max(2, 2 * rows_dev // owners)
    whole = lax.all_gather(tokens, "tp", axis=2, tiled=True)
    flattened = whole.reshape(rows_dev * decode_steps, whole.shape[2])
    piece = lax.all_gather(kv_weight, "fsdp", axis=0, tiled=True)
    base_terms = jnp.dot(
        flattened,
        piece.reshape(piece.shape[0], heads_per_shard * rotary_pair_width),
        preferred_element_type=jnp.float32,
    )
    owner = adapter_id // ADP_DEV
    earlier = (
        jnp.arange(rows_dev, dtype=jnp.int32)[:, None]
        > jnp.arange(rows_dev, dtype=jnp.int32)[None, :]
    )
    shared_owner = owner[:, None] == owner[None, :]
    rank_in = jnp.sum((shared_owner & earlier).astype(jnp.int32), axis=1)
    target = owner * capacity + rank_in
    outgoing = (
        jnp.zeros((owners * capacity, decode_steps, half_width), jnp.bfloat16)
        .at[target]
        .set(tokens)
    )
    labels = jnp.full((owners * capacity,), -1, jnp.int32).at[target].set(adapter_id)
    first = lax.axis_index(("fsdp", "rows")) * ADP_DEV
    catalog = jnp.arange(ADP_DEV, dtype=jnp.int32)
    names = lax.all_to_all(
        labels.reshape(owners, capacity), ("fsdp", "rows"), split_axis=0, concat_axis=0, tiled=True
    )
    leading_dims = names.shape
    chosen = (names[..., None] - first == catalog).astype(jnp.bfloat16)
    projected = jnp.einsum(
        "...sd,ard->...sar",
        lax.all_to_all(
            outgoing.reshape(owners, capacity, decode_steps, half_width),
            ("fsdp", "rows"),
            split_axis=0,
            concat_axis=0,
            tiled=True,
        ),
        adapter_a,
        preferred_element_type=jnp.float32,
    )
    position_coords = jnp.sum(projected * chosen.astype(jnp.float32)[..., None, :, None], axis=-2)
    position_coords = lax.psum(position_coords, "tp").astype(jnp.bfloat16)
    position_coords = position_coords.reshape(leading_dims + (decode_steps, 2, rank_size))
    spread = position_coords[..., None, :, :] * chosen[..., None, :, None, None]
    update_terms = jnp.einsum(
        "...sakr,akrhd->...shkd", spread, adapter_b, preferred_element_type=jnp.float32
    )
    returned = lax.all_to_all(
        (update_terms * low_rank_scale)
        .reshape(leading_dims + (decode_steps, heads_per_shard, rotary_pair_width))
        .astype(jnp.bfloat16),
        ("fsdp", "rows"),
        split_axis=0,
        concat_axis=0,
        tiled=True,
    )
    moved = returned.reshape(owners * capacity, decode_steps, heads_per_shard, rotary_pair_width)[
        target
    ]
    summed = base_terms.reshape(
        rows_dev, decode_steps, heads_per_shard, rotary_pair_width
    ) + moved.astype(jnp.float32)
    positions = (kv_len[:, None] + jnp.arange(decode_steps, dtype=jnp.int32)[None, :]).astype(
        jnp.float32
    )
    new_kv = rotate_keys(summed, positions).astype(jnp.bfloat16)
    attended = attend(queries, kv_cache, new_kv, kv_len)
    return (attended, new_kv)


def solution(mesh):
    placed = (
        P(("groups", "fsdp", "rows"), None, "tp"),
        P(("groups", "fsdp", "rows"), None, "tp", None),
        P(("groups", "fsdp", "rows"), None, "tp", None),
        P("fsdp", "tp", None),
        P(("fsdp", "rows"), None, "tp"),
        P(("fsdp", "rows"), None, None, "tp", None),
        P(("groups", "fsdp", "rows")),
        P(("groups", "fsdp", "rows")),
    )
    return jax.shard_map(
        local,
        mesh=mesh,
        in_specs=placed,
        out_specs=(
            P(("groups", "fsdp", "rows"), None, "tp", None),
            P(("groups", "fsdp", "rows"), None, "tp", None),
        ),
        check_vma=False,
    )
```

profile of v0, /device:TPU:14, one launch (start us, length us, event | category | flops | bytes accessed | tf_op | source)
XLA Modules:
  0.0 436.0 jit_solution(6250943104056108569)
XLA Ops:
  7.2 0.0 copy-start
  7.2 0.0 copy-start.5
  7.2 0.0 all-gather.5.cloned.1.call-start
  7.2 0.7 all-gather.5.cloned.1.call-update
  7.9 0.0 copy-done.5
  7.9 0.2 convert_reduce_fusion
  8.1 0.7 scatter_custom_fusion.1
  8.9 0.7 all_to_all.13
  9.6 6.2 %all-to-all-start.1 = ((s32[8,1,12]{2,1,0:T(1,128)}), s32[8,1,12]{2,1,0:T(1,128)S(1)}, u32[]{:S(2)}, u32[]{:S(2)}) async-start(s32[8,1,12]{2,1,0:T(1,128)} %bitcast.14), calls=%async_computation.1 | async-start | bytes 8192 | tf_op jit(solution)/shard_map/all_to_all | solution.py:106
  15.8 0.0 copy-start.1
  15.8 3.2 broadcast_in_dim.25
  19.0 0.0 copy-done.1
  19.0 7.2 %scatter_fusion = bf16[96,4,4096]{2,1,0:T(4,128)(2,1)} fusion(bf16[96,4,4096]{2,1,0:T(4,128)(2,1)} %broadcast_in_dim.25, s32[48]{0:T(128)S(1)} %compare_select_fusion, bf16[48,4,4096]{2,1,0:T(4,128)(2,1)S(1)} %copy-done.1), kind=kCustom, calls=%fused_computation.1 | custom fusion | bytes 4718784 | tf_op jit(solution)/shard_map/scatter | solution.py:101
  26.2 0.0 all-to-all-done.1
  26.2 6.0 %all-to-all-start = ((bf16[8,12,4,4096]{3,2,1,0:T(4,128)(2,1)}), bf16[8,12,4,4096]{3,2,1,0:T(4,128)(2,1)}, u32[]{:S(2)}, u32[]{:S(2)}) async-start(bf16[8,12,4,4096]{3,2,1,0:T(4,128)(2,1)} %bitcast.89), calls=%async_computation | async-start | bytes 6291456 | tf_op jit(solution)/shard_map/all_to_all | solution.py:113
  32.2 0.0 all-gather.3.cloned.1.call-start
  32.2 2.1 copy.79
  34.2 0.0 all-gather.3.cloned.1.call-update
  34.3 146.5 %all-to-all-done = bf16[8,12,4,4096]{3,2,1,0:T(4,128)(2,1)} async-done(((bf16[8,12,4,4096]{3,2,1,0:T(4,128)(2,1)}), bf16[8,12,4,4096]{3,2,1,0:T(4,128)(2,1)}, u32[]{:S(2)}, u32[]{:S(2)}) %all-to-all-start) | async-done | bytes 3145760 | tf_op jit(solution)/shard_map/all_to_all | solution.py:113
  180.8 0.0 copy-start.4
  180.8 11.7 %multiply_reduce_fusion = f32[8,12,4,32]{3,1,2,0:T(8,128)S(1)} fusion(bf16[16,32,4096]{2,1,0:T(8,128)(2,1)} %param.12, bf16[8,12,4,4096,1]{3,2,1,0,4:T(4,128)(2,1)} %bitcast.11, f32[8,12,16]{1,2,0:T(8,128)S(1)} %get-tuple-element.16), kind=kOutput, calls=%fused_computation.11 | convolution fusion | flops 1610993664 | bytes 7395328 | tf_op jit(solution)/shard_map/...sd,ard->...sar/dot_general | solution.py:111
  192.5 0.1 copy.84
  192.6 4.0 psum.7
  196.6 0.1 mul.124
  196.7 0.1 copy.85
  196.8 0.0 copy-done.4
  196.8 1.7 fusion.22
  198.6 0.8 copy.112
  199.4 0.0 copy-start.3
  199.4 1.4 reshape.155
  200.8 8.1 %all-to-all-start.2 = ((bf16[8,12,4,4,256]{4,3,2,1,0:T(4,128)(2,1)}), bf16[8,12,4,4,256]{4,3,2,1,0:T(4,128)(2,1)S(1)}, u32[]{:S(2)}, u32[]{:S(2)}) async-start(bf16[8,12,4,4,256]{4,3,2,1,0:T(4,128)(2,1)} %reshape.155), calls=%async_computation.2 | async-start | bytes 1572864 | tf_op jit(solution)/shard_map/all_to_all | solution.py:130
  208.9 0.0 copy-done.3
  208.9 0.1 iota_compare_fusion.2
  209.0 1.1 multiply_cosine_fusion
  210.1 3.2 fusion.43
  213.3 0.0 copy-done
  213.3 2.3 fusion.44
  215.6 41.1 %all-to-all-done.2 = bf16[8,12,4,4,256]{4,3,2,1,0:T(4,128)(2,1)S(1)} async-done(((bf16[8,12,4,4,256]{4,3,2,1,0:T(4,128)(2,1)}), bf16[8,12,4,4,256]{4,3,2,1,0:T(4,128)(2,1)S(1)}, u32[]{:S(2)}, u32[]{:S(2)}) %all-to-all-start.2) | async-done | bytes 786464 | tf_op jit(solution)/shard_map/all_to_all | solution.py:130
  256.7 1.6 gather_fusion
  258.4 119.1 %all-gather.5.cloned.1.call-done = bf16[8192,4,256]{2,1,0:T(4,128)(2,1)} async-done(((bf16[2048,4,256]{2,1,0:T(4,128)(2,1)}), bf16[8192,4,256]{2,1,0:T(4,128)(2,1)}) %all-gather.5.cloned.1.call-update) | async-done | bytes 16777232 | tf_op jit(solution)/shard_map/all_gather | solution.py:84
  377.5 26.5 %copy.107 = bf16[8192,4,256]{0,2,1:T(8,128)(2,1)} copy(bf16[8192,4,256]{2,1,0:T(4,128)(2,1)} %all-gather.5.cloned.1.call-done) | data formatting | bytes 33554432 | tf_op jit(solution)/shard_map/reshape | solution.py:87
  404.0 0.0 all-gather.3.cloned.1.call-done
  404.0 12.3 %fusion.25 = f32[48,4,4,256]{3,0,2,1:T(8,128)S(1)} fusion(bf16[8192,4,256]{0,2,1:T(8,128)(2,1)} %copy.107, bf16[48,4,8192]{2,0,1:T(8,128)(2,1)} %all-gather.3.cloned.1.call-done, bf16[48,4,4,256]{3,2,1,0:T(4,128)(2,1)} %gather_fusion), kind=kOutput, calls=%fused_computation.29 | convolution fusion | flops 3221618688 | bytes 21102592 | tf_op jit(solution)/shard_map/dot_general | solution.py:85
  416.4 1.1 subtract_convert_fusion
  417.5 0.1 maximum_bitcast_fusion
  417.6 0.2 pad_maximum_fusion
  417.8 0.9 copy.96
  418.8 0.0 copy-start.2
  418.8 1.4 fusion.45
  420.2 0.1 reduce_max.22
  420.3 0.0 copy-done.2
  420.3 2.9 fusion.42
  423.3 2.8 divide_convert_fusion
  426.0 0.6 fusion.17
  426.6 0.9 fusion.19
  427.5 0.5 copy.94
  428.1 1.1 copy.95
  (10 shorter events, 0.1 us)
Async XLA Ops:
  7.2 206.2 %copy-start = (bf16[48,4,16,128]{3,2,1,0:T(8,128)(2,1)S(1)}, bf16[48,4,16,128]{3,2,1,0:T(8,128)(2,1)}, u32[]{:S(2)}) copy-start(bf16[48,4,16,128]{3,2,1,0:T(8,128)(2,1)} %param.9) | copy-start | bytes 2359300
  7.2 0.7 copy-start.5
  7.2 370.3 %all-gather.5.cloned.1.call-start = ((), (), s32[]{:S(2)}) async-start(), calls=%async_computation.4 | async-start | bytes 20971520 | tf_op jit(solution)/shard_map/all_gather | solution.py:84
  9.6 16.6 %all-to-all-start.1 = ((s32[8,1,12]{2,1,0:T(1,128)}), s32[8,1,12]{2,1,0:T(1,128)S(1)}, u32[]{:S(2)}, u32[]{:S(2)}) async-start(s32[8,1,12]{2,1,0:T(1,128)} %bitcast.14), calls=%async_computation.1 | async-start | bytes 8192 | tf_op jit(solution)/shard_map/all_to_all | solution.py:106
  15.8 3.2 copy-start.1
  26.2 154.6 %all-to-all-start = ((bf16[8,12,4,4096]{3,2,1,0:T(4,128)(2,1)}), bf16[8,12,4,4096]{3,2,1,0:T(4,128)(2,1)}, u32[]{:S(2)}, u32[]{:S(2)}) async-start(bf16[8,12,4,4096]{3,2,1,0:T(4,128)(2,1)} %bitcast.89), calls=%async_computation | async-start | bytes 6291456 | tf_op jit(solution)/shard_map/all_to_all | solution.py:113
  32.2 371.8 %all-gather.3.cloned.1.call-start = ((), (), s32[]{:S(2)}) async-start(), calls=%async_computation.3 | async-start | bytes 4718592 | tf_op jit(solution)/shard_map/all_gather | solution.py:82
  180.8 16.1 %copy-start.4 = (bf16[16,2,16,4,128]{4,3,2,1,0:T(4,128)(2,1)S(1)}, bf16[16,2,16,4,128]{4,3,2,1,0:T(4,128)(2,1)}, u32[]{:S(2)}) copy-start(bf16[16,2,16,4,128]{4,3,2,1,0:T(4,128)(2,1)} %param.13) | copy-start | bytes 1572868
  199.4 9.5 %copy-start.3 = (s32[48]{0:T(128)S(1)}, s32[48]{0:T(128)}, u32[]{:S(2)}) copy-start(s32[48]{0:T(128)} %param.15) | copy-start | bytes 580
  200.8 56.0 %all-to-all-start.2 = ((bf16[8,12,4,4,256]{4,3,2,1,0:T(4,128)(2,1)}), bf16[8,12,4,4,256]{4,3,2,1,0:T(4,128)(2,1)S(1)}, u32[]{:S(2)}, u32[]{:S(2)}) async-start(bf16[8,12,4,4,256]{4,3,2,1,0:T(4,128)(2,1)} %reshape.155), calls=%async_computation.2 | async-start | bytes 1572864 | tf_op jit(solution)/shard_map/all_to_all | solution.py:130
  418.8 1.5 copy-start.2
Sparse Core Ops, SparseCore 0:
  9.6 367.8 all-gather.4
  379.1 14.4 all-gather.2
where the time goes:
time: 443 us; the launch traced here: 436 us
  waiting for transfers between devices  307 us (69%)
  local copies, waits for them, and re-layouts  50.4 us (11%)
  matrix products  30.9 us (7%)
  starting transfers between devices  20.4 us (5%)
  between operations  14.3 us (3%)
  other arithmetic  8.68 us (2%)
    all_to_all x1, waiting for transfers between devices, local(): lax.all_to_all(outgoing.reshape(owners, capacity, decode_steps, half_widt...  146 us
    all_gather x1, waiting for transfers between devices, local(): piece = lax.all_gather(kv_weight, 'fsdp', axis=0, tiled=True)  119 us
    all_to_all x1, waiting for transfers between devices, local(): lax.all_to_all((update_terms * low_rank_scale).reshape(leading_dims + (de...  41.1 us
    reshape x1, local copies, waits for them, and re-layouts, local(): piece.reshape(piece.shape[0], heads_per_shard * rotary_pair_width)  26.5 us
    dot_general x1, matrix products, local(): jnp.dot(flattened, piece.reshape(piece.shape[0], heads_per_shard * rotary...  12.3 us
    dot_general x1, matrix products, local(): jnp.einsum('...sd,ard->...sar', lax.all_to_all(outgoing.reshape(owners, c...  11.7 us
  transfers between devices with their start and end apart: 5, of which 3 were waited for; matrix products, arithmetic and copies ran while one was open for 15% of the time, Pallas kernels for 0%

commit v1 on v0

v1 whole, which is shorter than its diff:
```python
import functools
import math

import jax
import jax.numpy as jnp
from jax import lax
from jax.experimental import pallas as pl
from jax.experimental.pallas import tpu as pltpu
from jax.sharding import PartitionSpec as P

ADP_DEV = 16
CHUNKS = 4
MESH = pl.DeviceIdType.MESH

low_rank_scale = 0.5
rope_base = 500000.0


def rotate_keys(summed, positions):
    depth = summed.shape[-1] // 2
    half = depth // 2
    index = jnp.arange(half, dtype=jnp.int32).astype(jnp.float32)
    inverse = jnp.exp(index * (-2.0 * math.log(rope_base) / depth))
    angle = positions[..., None] * inverse
    cosine = jnp.cos(angle)[:, :, None, :]
    sine = jnp.sin(angle)[:, :, None, :]
    first = summed[..., :half]
    second = summed[..., half:depth]
    return jnp.concatenate(
        [first * cosine - second * sine, second * cosine + first * sine, summed[..., depth:]],
        axis=-1,
    )


def attend(queries, cache, fresh, lengths):
    batch, decode_steps, query_heads, depth = queries.shape
    kv_heads = cache.shape[2]
    context = cache.shape[1]
    grouped = queries.reshape(batch, decode_steps, kv_heads, query_heads // kv_heads, depth)
    scale = 1.0 / math.sqrt(depth)
    older = (
        jnp.einsum(
            "rsgqd,rpgd->rsgqp", grouped, cache[..., :depth], preferred_element_type=jnp.float32
        )
        * scale
    )
    newer = (
        jnp.einsum(
            "rsgqd,rtgd->rsgqt", grouped, fresh[..., :depth], preferred_element_type=jnp.float32
        )
        * scale
    )
    visible_old = jnp.arange(context, dtype=jnp.int32)[None, :] < lengths[:, None]
    visible_new = (
        jnp.arange(decode_steps, dtype=jnp.int32)[None, :]
        <= jnp.arange(decode_steps, dtype=jnp.int32)[:, None]
    )
    older = jnp.where(visible_old[:, None, None, None, :], older, -jnp.inf)
    newer = jnp.where(visible_new[None, :, None, None, :], newer, -jnp.inf)
    scores = jnp.concatenate([older, newer], axis=-1)
    top = jnp.max(scores, axis=-1, keepdims=True)
    weights = jnp.exp(scores - top)
    weights = (weights / jnp.sum(weights, axis=-1, keepdims=True)).astype(jnp.bfloat16)
    mixed = jnp.einsum(
        "rsgqp,rpgd->rsgqd",
        weights[..., :context],
        cache[..., depth:],
        preferred_element_type=jnp.float32,
    )
    mixed = mixed + jnp.einsum(
        "rsgqt,rtgd->rsgqd",
        weights[..., context:],
        fresh[..., depth:],
        preferred_element_type=jnp.float32,
    )
    return mixed.reshape(batch, decode_steps, query_heads, depth).astype(jnp.bfloat16)


def gather_kernel(
    n, m, tok, a, b, ids, tok_all, slices, a_all, b_all, ids_all,
    own_sem, right_send, left_send, tok_recv, core_send, core_recv,
    x_send, x_recv, id_send, id_recv,
):
    f = lax.axis_index("fsdp")
    r = lax.axis_index("rows")
    t = lax.axis_index("tp")
    rows, half = tok.shape
    part = rows // CHUNKS
    width = slices.shape[2]
    per_core = half // width
    holds = t == f // per_core
    column = pl.multiple_of(lax.rem(f, per_core) * width, width)

    barrier = pltpu.get_barrier_semaphore()
    for k in range(1, n):
        pl.semaphore_signal(
            barrier, inc=1, device_id={"fsdp": lax.rem(f + k, n)}, device_id_type=MESH
        )
    for k in range(1, m):
        pl.semaphore_signal(
            barrier, inc=1, device_id={"rows": lax.rem(r + k, m)}, device_id_type=MESH
        )
    pl.semaphore_signal(barrier, inc=1, device_id={"tp": 1 - t}, device_id_type=MESH)
    pl.semaphore_wait(barrier, n + m - 1)

    def piece(c):
        return pl.ds(c * part, part)

    def along(source, src, c, to, sems):
        return pltpu.make_async_remote_copy(
            src_ref=source,
            dst_ref=tok_all.at[src, piece(c)],
            send_sem=sems.at[src, c],
            recv_sem=tok_recv.at[src, c],
            device_id={"fsdp": to},
            device_id_type=MESH,
        )

    def across(source, src, c):
        return pltpu.make_async_remote_copy(
            src_ref=source,
            dst_ref=slices.at[src, piece(c)],
            send_sem=core_send.at[src, c],
            recv_sem=core_recv.at[src, c],
            device_id={"tp": 1 - t},
            device_id_type=MESH,
        )

    def keep(source, src, c):
        return pltpu.make_async_copy(source, slices.at[src, piece(c)], core_recv.at[src, c])

    def id_copy(k):
        return pltpu.make_async_remote_copy(
            src_ref=ids,
            dst_ref=ids_all.at[f],
            send_sem=id_send.at[k],
            recv_sem=id_recv.at[k],
            device_id={"fsdp": lax.rem(f + k, n)},
            device_id_type=MESH,
        )

    def x_copy(k, which):
        source, target = ((a, a_all), (b, b_all))[which]
        return pltpu.make_async_remote_copy(
            src_ref=source,
            dst_ref=target.at[r],
            send_sem=x_send.at[which, k],
            recv_sem=x_recv.at[which, k],
            device_id={"rows": lax.rem(r + k, m)},
            device_id_type=MESH,
        )

    for c in range(CHUNKS):
        @pl.when(f < n - 1)
        def _():
            along(tok.at[piece(c)], f, c, f + 1, right_send).start()

        @pl.when(f > 0)
        def _():
            along(tok.at[piece(c)], f, c, f - 1, left_send).start()

    for k in range(1, n):
        id_copy(k).start()
    for k in range(1, m):
        for which in range(2):
            x_copy(k, which).start()
    locals_ = [
        pltpu.make_async_copy(tok, tok_all.at[f], own_sem.at[0]),
        pltpu.make_async_copy(a, a_all.at[r], own_sem.at[1]),
        pltpu.make_async_copy(b, b_all.at[r], own_sem.at[2]),
        pltpu.make_async_copy(ids, ids_all.at[f], own_sem.at[3]),
    ]
    for copy in locals_:
        copy.start()
    for c in range(CHUNKS):
        @pl.when(holds)
        def _():
            across(tok.at[piece(c), pl.ds(column, width)], f, c).start()
            keep(tok.at[piece(c), pl.ds(column, width)], f, c).start()

    for d in range(1, n):
        for c in range(CHUNKS):
            @pl.when(f >= d)
            def _():
                src = f - d
                along(tok.at[piece(c)], src, c, f, right_send).wait_recv()

                @pl.when(f < n - 1)
                def _():
                    along(tok_all.at[src, piece(c)], src, c, f + 1, right_send).start()

                @pl.when(holds)
                def _():
                    across(tok_all.at[src, piece(c), pl.ds(column, width)], src, c).start()
                    keep(tok_all.at[src, piece(c), pl.ds(column, width)], src, c).start()

            @pl.when(f + d < n)
            def _():
                src = f + d
                along(tok.at[piece(c)], src, c, f, left_send).wait_recv()

                @pl.when(f > 0)
                def _():
                    along(tok_all.at[src, piece(c)], src, c, f - 1, left_send).start()

                @pl.when(holds)
                def _():
                    across(tok_all.at[src, piece(c), pl.ds(column, width)], src, c).start()
                    keep(tok_all.at[src, piece(c), pl.ds(column, width)], src, c).start()

    for copy in locals_:
        copy.wait()
    for k in range(1, n):
        id_copy(k).wait()
    for k in range(1, m):
        for which in range(2):
            x_copy(k, which).wait()
    for src in range(n):
        for c in range(CHUNKS):
            @pl.when(jnp.logical_and(src <= f, f < n - 1))
            def _():
                along(tok.at[piece(c)], src, c, f, right_send).wait_send()

            @pl.when(jnp.logical_and(src >= f, f > 0))
            def _():
                along(tok.at[piece(c)], src, c, f, left_send).wait_send()

            @pl.when(holds)
            def _():
                across(tok.at[piece(c), pl.ds(column, width)], src, c).wait_send()
                keep(tok.at[piece(c), pl.ds(column, width)], src, c).wait()

            @pl.when(jnp.logical_not(holds))
            def _():
                across(tok.at[piece(c), pl.ds(column, width)], src, c).wait_recv()


def gather(tok, a, b, ids, n, m, width):
    shape = jax.ShapeDtypeStruct
    anywhere = pl.BlockSpec(memory_space=pl.ANY)
    dma = pltpu.SemaphoreType.DMA
    return pl.pallas_call(
        functools.partial(gather_kernel, n, m),
        out_shape=(
            shape((n,) + tok.shape, tok.dtype),
            shape((n, tok.shape[0], width), tok.dtype),
            shape((m,) + a.shape, a.dtype),
            shape((m,) + b.shape, b.dtype),
            shape((n,) + ids.shape, ids.dtype),
        ),
        in_specs=[anywhere] * 4,
        out_specs=[anywhere] * 5,
        scratch_shapes=[
            dma((4,)),
            dma((n, CHUNKS)),
            dma((n, CHUNKS)),
            dma((n, CHUNKS)),
            dma((n, CHUNKS)),
            dma((n, CHUNKS)),
            dma((2, m)),
            dma((2, m)),
            dma((n,)),
            dma((n,)),
        ],
        compiler_params=pltpu.CompilerParams(collective_id=0, has_side_effects=True),
    )(tok, a, b, ids)


def exchange_kernel(n, parts, out, send, recv):
    f = lax.axis_index("fsdp")
    barrier = pltpu.get_barrier_semaphore()
    for k in range(1, n):
        pl.semaphore_signal(
            barrier, inc=1, device_id={"fsdp": lax.rem(f + k, n)}, device_id_type=MESH
        )
    pl.semaphore_wait(barrier, n - 1)

    def copy(k):
        to = lax.rem(f + k, n)
        return pltpu.make_async_remote_copy(
            src_ref=parts.at[to],
            dst_ref=out.at[f],
            send_sem=send.at[k],
            recv_sem=recv.at[k],
            device_id={"fsdp": to},
            device_id_type=MESH,
        )

    for k in range(1, n):
        copy(k).start()
    for k in range(1, n):
        copy(k).wait()


def exchange(parts, n):
    anywhere = pl.BlockSpec(memory_space=pl.ANY)
    return pl.pallas_call(
        functools.partial(exchange_kernel, n),
        out_shape=jax.ShapeDtypeStruct(parts.shape, parts.dtype),
        in_specs=[anywhere],
        out_specs=anywhere,
        scratch_shapes=[pltpu.SemaphoreType.DMA((n,)), pltpu.SemaphoreType.DMA((n,))],
        compiler_params=pltpu.CompilerParams(collective_id=1, has_side_effects=True),
    )(parts)


def local(tokens, queries, kv_cache, kv_weight, adapter_a, adapter_b, adapter_id, kv_len):
    n = lax.axis_size("fsdp")
    m = lax.axis_size("rows")
    f = lax.axis_index("fsdp")
    rows_dev, decode_steps, half_width = tokens.shape
    width, heads, pair = kv_weight.shape
    rank = adapter_b.shape[2]
    count = rows_dev * decode_steps
    known = m * ADP_DEV

    flat = tokens.reshape(count, half_width)
    weight = kv_weight.reshape(width, heads * pair)
    down = adapter_a.reshape(ADP_DEV * 2 * rank, half_width)
    up = adapter_b.reshape(ADP_DEV * 2 * rank, heads * (pair // 2))
    lanes = -(-rows_dev // 128) * 128
    ids = jnp.broadcast_to(jnp.pad(adapter_id, (0, lanes - rows_dev))[None, :], (8, lanes))
    tok_all, slices, a_all, b_all, ids_all = gather(flat, down, up, ids, n, m, width)

    names = ids_all[:, 0, :rows_dev].reshape(n * rows_dev) - f * known
    chosen = names[:, None] == jnp.arange(known, dtype=jnp.int32)
    chosen = jnp.broadcast_to(chosen[:, None, :], (n * rows_dev, decode_steps, known))
    chosen = chosen.reshape(n * count, known)
    projected = lax.dot_general(
        tok_all.reshape(n * count, half_width),
        a_all.reshape(known * 2 * rank, half_width),
        (((1,), (1,)), ((), ())),
        preferred_element_type=jnp.float32,
    )
    coords = jnp.sum(
        jnp.where(chosen[:, :, None], projected.reshape(n * count, known, 2 * rank), 0.0), axis=1
    )
    coords = lax.psum(coords, "tp").astype(jnp.bfloat16)
    spread = jnp.where(chosen[:, :, None], coords[:, None, :], jnp.bfloat16(0))
    spread = spread.reshape(n * count, known, 2, rank)
    delta = jnp.einsum(
        "takr,akrhd->thkd",
        spread,
        b_all.reshape(known, 2, rank, heads, pair // 2),
        preferred_element_type=jnp.float32,
    )
    delta = (delta * low_rank_scale).astype(jnp.bfloat16).reshape(n * count, heads * pair)
    partial = jnp.dot(
        slices.reshape(n * count, width), weight, preferred_element_type=jnp.float32
    )
    partial = (partial + delta.astype(jnp.float32)).reshape(n, count, heads * pair)
    others = exchange(partial.astype(jnp.bfloat16), n)
    mine = lax.dynamic_index_in_dim(partial, f, 0, keepdims=False)
    slot = jnp.arange(n, dtype=jnp.int32)[:, None, None]
    summed = mine + jnp.sum(jnp.where(slot == f, 0.0, others.astype(jnp.float32)), axis=0)
    summed = summed.reshape(rows_dev, decode_steps, heads, pair)
    positions = (kv_len[:, None] + jnp.arange(decode_steps, dtype=jnp.int32)[None, :]).astype(
        jnp.float32
    )
    new_kv = rotate_keys(summed, positions).astype(jnp.bfloat16)
    attended = attend(queries, kv_cache, new_kv, kv_len)
    return (attended, new_kv)


def solution(mesh):
    placed = (
        P(("groups", "fsdp", "rows"), None, "tp"),
        P(("groups", "fsdp", "rows"), None, "tp", None),
        P(("groups", "fsdp", "rows"), None, "tp", None),
        P("fsdp", "tp", None),
        P(("fsdp", "rows"), None, "tp"),
        P(("fsdp", "rows"), None, None, "tp", None),
        P(("groups", "fsdp", "rows")),
        P(("groups", "fsdp", "rows")),
    )
    return jax.shard_map(
        local,
        mesh=mesh,
        in_specs=placed,
        out_specs=(
            P(("groups", "fsdp", "rows"), None, "tp", None),
            P(("groups", "fsdp", "rows"), None, "tp", None),
        ),
        check_vma=False,
    )
```

time: 443 us -> 400 us (0.903); the launches traced: 436 us -> 399 us
  Pallas kernels: 0 us -> 329 us
  waiting for transfers between devices: 307 us -> 0 us
  local copies, waits for them, and re-layouts: 50.4 us -> 27.7 us
  starting transfers between devices: 20.4 us -> 0 us
  between operations: 14.3 us -> 0.9 us
  matrix products: 30.9 us -> 24 us
  other arithmetic: 8.68 us -> 14.2 us
    pallas_call x0 -> x2, Pallas kernels: none -> 329 us  [the longest x1 291 us: gather(): pl.pallas_call(functools.partial(gather_kernel, n, m), out_shape=(shape((...]
    all_to_all x3 -> x0, waiting for transfers between devices: 188 us -> none  [the longest x1 146 us: local(): lax.all_to_all(outgoing.reshape(owners, capacity, decode_steps, half_widt...]
    all_gather x2 -> x0, waiting for transfers between devices: 119 us -> none  [the longest x1 119 us: local(): piece = lax.all_gather(kv_weight, 'fsdp', axis=0, tiled=True)]
    reshape x1 -> x2, local copies, waits for them, and re-layouts: 26.5 us -> 3.87 us  [the longest x1 3.58 us: local(): flat = tokens.reshape(count, half_width)]
    all_to_all x3 -> x0, starting transfers between devices: 20.3 us -> none  [the longest x1 8.11 us: local(): lax.all_to_all((update_terms * low_rank_scale).reshape(leading_dims + (de...]
    convert_element_type x2, local copies, waits for them, and re-layouts: 2.19 us -> 11.3 us  [local(): delta.astype(jnp.float32)]
    scatter x2 -> x0, local copies, waits for them, and re-layouts: 7.88 us -> none  [the longest x1 7.15 us: local(): outgoing = jnp.zeros((owners * capacity, decode_steps, half_width), jnp.b...]
    dot_general x3, matrix products: 25.7 us -> 19.7 us  [the longest x1 11.1 us: local(): lax.dot_general(tok_all.reshape(n * count, half_width), a_all.reshape(kno...]
  transfers between devices with their start and end apart: 5 -> 0, of which waited for: 3 -> 0; matrix products, arithmetic and copies ran while one was open for 15% -> 0% of each run, Pallas kernels for 0% -> 0%
where the time goes in v1:
time: 400 us; the launch traced here: 399 us
  Pallas kernels  329 us (82%)
  local copies, waits for them, and re-layouts  27.7 us (7%)
  matrix products  24 us (6%)
  other arithmetic  14.2 us (4%)
    pallas_call x1, Pallas kernels, gather(): pl.pallas_call(functools.partial(gather_kernel, n, m), out_shape=(shape((...  291 us
    pallas_call x1, Pallas kernels, exchange(): pl.pallas_call(functools.partial(exchange_kernel, n), out_shape=jax.Shape...  38 us
    convert_element_type x2, local copies, waits for them, and re-layouts, local(): delta.astype(jnp.float32)  11.3 us
    dot_general x1, matrix products, local(): lax.dot_general(tok_all.reshape(n * count, half_width), a_all.reshape(kno...  11.1 us

profile of v1, /device:TPU:14, one launch (start us, length us, event | category | flops | bytes accessed | tf_op | source)
XLA Modules:
  0.0 399.0 jit_solution(16900621270726112477)
XLA Ops:
  0.6 0.0 copy-start
  0.6 0.0 copy-start.4
  0.7 0.0 copy-start.7
  0.7 3.6 reshape.143.tok
  4.2 0.0 copy-done.4
  4.3 0.9 copy.61
  5.1 0.0 copy-done.7
  5.1 0.6 broadcast_in_dim.105.ids
  5.7 290.6 %shard_map.95 = (bf16[4,192,4096]{2,1,0:T(8,128)(2,1)}, bf16[4,192,2048]{2,1,0:T(8,128)(2,1)}, bf16[2,512,4096]{2,1,0:T(8,128)(2,1)}, bf16[2,512,512]{2,1,0:T(8,128)(2,1)}, s32[4,8,128]{2,1,0:T(8,128)}) custom-call(bf16[192,4096]{1,0:T(8,128)(2,1)} %reshape.143.tok, bf16[512,4096]{1,0:T(8,128)(2,1)} %bitcast.76, bf16[512,512]{1,0:T(8,128)(2,1)} %bitcast.80, ...), custom_call_target="tpu_custom_call" | custom-call | tf_op jit(solution)/shard_map/pallas_call | solution.py:242
  296.3 0.7 subtract_reduce_fusion
  297.1 0.1 sub.26
  297.2 0.1 iota_compare_fusion
  297.3 0.1 broadcast_in_dim.106
  297.4 0.2 copy.19
  297.5 0.0 copy-start.3
  297.5 11.1 %select_reduce_fusion.1 = f32[768,32]{0,1:T(8,128)S(1)} fusion(bf16[768,4096,1]{1,0,2:T(8,128)(2,1)} %bitcast.85, bf16[32,32,4096]{2,1,0:T(8,128)(2,1)} %bitcast.84, pred[768,32]{0,1:T(8,128)(4,1)S(1)} %copy.19), kind=kOutput, calls=%fused_computation.4 | convolution fusion | flops 6443999232 | bytes 14802944 | tf_op jit(solution)/shard_map/dot_general | solution.py:329
  308.6 3.7 psum.7
  312.3 0.0 copy-done.3
  312.3 0.3 reshape.148
  312.6 3.6 convert_bitcast_fusion
  316.2 5.8 %copy.22 = f32[768,4,2,128]{3,2,1,0:T(2,128)} copy(f32[768,4,2,128]{0,3,1,2:T(8,128)} %convert_bitcast_fusion) | data formatting | bytes 6291456 | tf_op jit(solution)/shard_map/convert_element_type | solution.py:351
  321.9 5.5 %reshape.151 = f32[768,1024]{1,0:T(8,128)} reshape(f32[768,4,2,128]{3,2,1,0:T(2,128)} %copy.22) | data formatting | bytes 6291456 | tf_op jit(solution)/shard_map/convert_element_type | solution.py:351
  327.5 0.0 copy-start.2
  327.5 0.0 copy-start.6
  327.5 3.4 copy.39
  330.9 0.0 copy-done.2
  330.9 0.7 copy-done.6
  331.6 5.1 %convolution_add_fusion = f32[768,1024]{1,0:T(8,128)} fusion(f32[768,1024]{1,0:T(8,128)S(1)} %copy-done.2, bf16[768,2048]{1,0:T(8,128)(2,1)S(1)} %bitcast.86, bf16[2048,1024]{1,0:T(8,128)(2,1)S(1)} %bitcast.78), kind=kOutput, calls=%fused_computation.5 | convolution fusion | flops 3222011904 | bytes 13631488 | tf_op jit(solution)/shard_map/dot_general | solution.py:348
  336.7 1.2 constant_dynamic-slice_fusion
  337.9 0.4 squeeze.4
  338.2 3.3 convert_element_type.51.parts
  341.5 38.0 %shard_map.96 = bf16[4,192,1024]{2,1,0:T(8,128)(2,1)} custom-call(bf16[4,192,1024]{2,1,0:T(8,128)(2,1)} %convert_element_type.51.parts), custom_call_target="tpu_custom_call" | custom-call | tf_op jit(solution)/shard_map/pallas_call | solution.py:297
  379.5 1.9 select_reduce_fusion
  381.5 0.0 copy-start.5
  381.5 0.4 reduce_sum.31
  381.9 0.4 copy_add_fusion
  382.2 0.0 copy-done.5
  382.2 0.1 add_convert_fusion.1
  382.3 0.8 multiply_cosine_fusion
  383.1 0.4 subtract_convert_fusion
  383.5 0.1 slice.51
  383.6 0.5 pad_maximum_fusion
  384.0 0.9 copy.29
  384.9 0.0 copy-done
  384.9 0.0 copy-start.1
  384.9 1.6 fusion.23
  386.5 0.3 copy-done.1
  386.8 1.8 fusion.21
  388.6 0.1 iota_compare_fusion.1
  388.7 1.3 fusion.22
  390.0 0.1 reduce_max.22
  390.1 3.1 fusion.20
  393.2 2.8 divide_convert_fusion
  396.0 0.6 fusion.2
  396.6 0.9 fusion.5
  397.4 0.5 copy.27
  397.9 1.1 copy.28
  (4 shorter events, 0.0 us)
Async XLA Ops:
  0.6 384.3 %copy-start = (bf16[48,4,16,128]{3,2,1,0:T(8,128)(2,1)S(1)}, bf16[48,4,16,128]{3,2,1,0:T(8,128)(2,1)}, u32[]{:S(2)}) copy-start(bf16[48,4,16,128]{3,2,1,0:T(8,128)(2,1)} %param.9) | copy-start | bytes 2359300
  0.6 3.6 copy-start.4
  0.7 4.5 %copy-start.7 = (s32[48]{0:T(128)S(1)}, s32[48]{0:T(128)}, u32[]{:S(2)}) copy-start(s32[48]{0:T(128)} %param.14) | copy-start | bytes 580
  297.5 14.8 %copy-start.3 = (bf16[2,512,512]{2,1,0:T(8,128)(2,1)S(1)}, bf16[2,512,512]{2,1,0:T(8,128)(2,1)}, u32[]{:S(2)}) copy-start(bf16[2,512,512]{2,1,0:T(8,128)(2,1)} %get-tuple-element.8) | copy-start | bytes 3145732
  327.5 3.4 copy-start.2
  327.5 4.1 %copy-start.6 = (bf16[4,192,2048]{2,1,0:T(8,128)(2,1)S(1)}, bf16[4,192,2048]{2,1,0:T(8,128)(2,1)}, u32[]{:S(2)}) copy-start(bf16[4,192,2048]{2,1,0:T(8,128)(2,1)} %get-tuple-element.7) | copy-start | bytes 9437188
  381.5 0.8 copy-start.5
  384.9 1.9 copy-start.1

commit v2 on v1

--- a/solution.py
+++ b/solution.py
@@ -78,7 +78,7 @@
 
 def gather_kernel(
     n, m, tok, a, b, ids, tok_all, slices, a_all, b_all, ids_all,
-    own_sem, right_send, left_send, tok_recv, core_send, core_recv,
+    tok_v, a_v, b_v, ids_v, in_sem, own_sem, right_send, left_send, tok_recv, core_send, core_recv,
     x_send, x_recv, id_send, id_recv,
 ):
     f = lax.axis_index("fsdp")
@@ -164,19 +164,24 @@
     for k in range(1, m):
         for which in range(2):
             x_copy(k, which).start()
+    held = ((tok, tok_v), (a, a_v), (b, b_v), (ids, ids_v))
+    inward = [pltpu.make_async_copy(x, v, in_sem.at[i]) for i, (x, v) in enumerate(held)]
+    for copy in inward:
+        copy.start()
     locals_ = [
-        pltpu.make_async_copy(tok, tok_all.at[f], own_sem.at[0]),
-        pltpu.make_async_copy(a, a_all.at[r], own_sem.at[1]),
-        pltpu.make_async_copy(b, b_all.at[r], own_sem.at[2]),
-        pltpu.make_async_copy(ids, ids_all.at[f], own_sem.at[3]),
+        pltpu.make_async_copy(tok_v, tok_all.at[f], own_sem.at[0]),
+        pltpu.make_async_copy(a_v, a_all.at[r], own_sem.at[1]),
+        pltpu.make_async_copy(b_v, b_all.at[r], own_sem.at[2]),
+        pltpu.make_async_copy(ids_v, ids_all.at[f], own_sem.at[3]),
     ]
-    for copy in locals_:
-        copy.start()
+    for first, second in zip(inward, locals_):
+        first.wait()
+        second.start()
     for c in range(CHUNKS):
         @pl.when(holds)
         def _():
             across(tok.at[piece(c), pl.ds(column, width)], f, c).start()
-            keep(tok.at[piece(c), pl.ds(column, width)], f, c).start()
+            keep(tok_v.at[piece(c), pl.ds(column, width)], f, c).start()
 
     for d in range(1, n):
         for c in range(CHUNKS):
@@ -250,7 +255,9 @@
         ),
         in_specs=[anywhere] * 4,
         out_specs=[anywhere] * 5,
-        scratch_shapes=[
+        scratch_shapes=[pltpu.VMEM(x.shape, x.dtype) for x in (tok, a, b, ids)]
+        + [
+            dma((4,)),
             dma((4,)),
             dma((n, CHUNKS)),
             dma((n, CHUNKS)),
@@ -262,7 +269,9 @@
             dma((n,)),
             dma((n,)),
         ],
-        compiler_params=pltpu.CompilerParams(collective_id=0, has_side_effects=True),
+        compiler_params=pltpu.CompilerParams(
+            collective_id=0, has_side_effects=True, vmem_limit_bytes=32 * 2**20
+        ),
     )(tok, a, b, ids)
 
 

time: 400 us -> 219 us (0.55)
  Pallas kernels: 329 us -> 145 us
  local copies, waits for them, and re-layouts: 27.7 us -> 31.7 us
    pallas_call x1, Pallas kernels: 291 us -> 106 us  [gather(): pl.pallas_call(functools.partial(gather_kernel, n, m), out_shape=(shape((...]
    unnamed x20 -> x24, local copies, waits for them, and re-layouts: 7.28 us -> 13 us
where the time goes in v2:
time: 219 us
  Pallas kernels  145 us (66%)
  local copies, waits for them, and re-layouts  31.7 us (14%)
  matrix products  23.9 us (11%)
  other arithmetic  13.4 us (6%)
  blocking collectives  3.69 us (2%)
    pallas_call x1, Pallas kernels, gather(): pl.pallas_call(functools.partial(gather_kernel, n, m), out_shape=(shape((...  106 us
    pallas_call x1, Pallas kernels, exchange(): pl.pallas_call(functools.partial(exchange_kernel, n), out_shape=jax.Shape...  39.3 us
    unnamed x24, local copies, waits for them, and re-layouts  13 us
    convert_element_type x2, local copies, waits for them, and re-layouts, local(): delta.astype(jnp.float32)  11.3 us
    dot_general x1, matrix products, local(): lax.dot_general(tok_all.reshape(n * count, half_width), a_all.reshape(kno...  11 us
    dot_general x1, matrix products, local(): jnp.dot(slices.reshape(n * count, width), weight, preferred_element_type=...  5.09 us

profile of v2, /device:TPU:14, one launch (start us, length us, event | category | flops | bytes accessed | tf_op | source)
XLA Modules:
  0.0 218.6 jit_solution(14208231921294976774)
XLA Ops:
  0.6 0.0 copy-start
  0.6 0.0 copy-start.7
  0.7 0.0 copy-start.9
  0.7 2.5 %reshape.143.tok = bf16[192,4096]{1,0:T(8,128)(2,1)S(1)} reshape(bf16[48,4,4096]{2,1,0:T(4,128)(2,1)} %param.8) | data formatting | bytes 3145728 | tf_op jit(solution)/shard_map/reshape | solution.py:326
  3.1 0.0 copy-done.7
  3.1 0.1 copy.61
  3.2 0.0 copy-done.9
  3.3 0.0 copy-start.1
  3.3 2.2 copy-done.1
  5.4 105.7 %shard_map.95 = (bf16[4,192,4096]{2,1,0:T(8,128)(2,1)S(1)}, bf16[4,192,2048]{2,1,0:T(8,128)(2,1)S(1)}, bf16[2,512,4096]{2,1,0:T(8,128)(2,1)}, bf16[2,512,512]{2,1,0:T(8,128)(2,1)S(1)}, s32[4,8,128]{2,1,0:T(8,128)S(1)}) custom-call(bf16[192,4096]{1,0:T(8,128)(2,1)S(1)} %reshape.143.tok, bf16[512,4096]{1,0:T(8,128)(2,1)S(1)} %bitcast.74, ...), custom_call_target="tpu_custom_call" | custom-call | tf_op jit(solution)/shard_map/pallas_call | solution.py:247
  111.1 0.0 copy-start.2
  111.1 2.7 %copy-done.2 = bf16[4,192,4096]{2,1,0:T(8,128)(2,1)} copy-done((bf16[4,192,4096]{2,1,0:T(8,128)(2,1)}, bf16[4,192,4096]{2,1,0:T(8,128)(2,1)S(1)}, u32[]{:S(2)}) %copy-start.2) | copy-done | bytes 6291480
  113.8 0.0 copy-start.3
  113.8 1.6 copy-done.3
  115.5 0.1 sub.26
  115.6 0.1 iota_compare_fusion
  115.7 0.1 broadcast_in_dim.106
  115.8 0.2 copy.19
  115.9 11.0 %select_reduce_fusion.1 = f32[768,32]{0,1:T(8,128)S(1)} fusion(bf16[768,4096,1]{1,0,2:T(8,128)(2,1)} %bitcast.76, bf16[32,32,4096]{2,1,0:T(8,128)(2,1)} %bitcast.86, pred[768,32]{0,1:T(8,128)(4,1)S(1)} %copy.19), kind=kOutput, calls=%fused_computation.4 | convolution fusion | flops 6443999232 | bytes 14802944 | tf_op jit(solution)/shard_map/dot_general | solution.py:338
  126.9 3.7 %psum.7 = bf16[768,32]{0,1:T(8,128)(2,1)S(1)} all-reduce(f32[768,32]{0,1:T(8,128)S(1)} %select_reduce_fusion.1), channel_id=1, replica_groups=mesh['groups'=2,'fsdp'=4,'rows'=2,'tp'=2] {'tp'}, use_global_device_ids=true, to_apply=%region_1.2 | all-reduce | flops 24576 | bytes 147456 | tf_op jit(solution)/shard_map/psum | solution.py:347
  130.6 0.3 reshape.148
  130.9 3.5 %convert_bitcast_fusion = f32[768,4,2,128]{0,3,1,2:T(8,128)} fusion(pred[768,32]{0,1:T(8,128)(4,1)S(1)} %copy.19, bf16[32,2,16,4,128]{4,3,2,1,0:T(4,128)(2,1)S(1)} %reshape.148, bf16[768,2,16]{0,2,1:T(8,128)(2,1)S(1)} %bitcast.85), kind=kOutput, calls=%fused_computation.2 | convolution fusion | flops 808452096 | bytes 4268032 | tf_op jit(solution)/shard_map/takr,akrhd->thkd/dot_general | solution.py:350
  134.4 5.8 %copy.22 = f32[768,4,2,128]{3,2,1,0:T(2,128)} copy(f32[768,4,2,128]{0,3,1,2:T(8,128)} %convert_bitcast_fusion) | data formatting | bytes 6291456 | tf_op jit(solution)/shard_map/convert_element_type | solution.py:360
  140.2 5.5 %reshape.151 = f32[768,1024]{1,0:T(8,128)} reshape(f32[768,4,2,128]{3,2,1,0:T(2,128)} %copy.22) | data formatting | bytes 6291456 | tf_op jit(solution)/shard_map/convert_element_type | solution.py:360
  145.7 0.0 copy-start.4
  145.7 0.0 copy-start.6
  145.7 3.4 %copy.39 = bf16[256,8,4,256]{3,1,2,0:T(8,128)(2,1)S(1)} copy(bf16[256,8,4,256]{3,2,1,0:T(4,128)(2,1)} %bitcast.80) | data formatting | bytes 8388608
  149.1 0.0 copy-done.4
  149.1 0.7 copy-done.6
  149.8 5.1 %convolution_add_fusion = f32[768,1024]{1,0:T(8,128)} fusion(f32[768,1024]{1,0:T(8,128)S(1)} %copy-done.6, bf16[768,2048]{1,0:T(8,128)(2,1)S(1)} %bitcast.77, bf16[2048,1024]{1,0:T(8,128)(2,1)S(1)} %bitcast.81), kind=kOutput, calls=%fused_computation.5 | convolution fusion | flops 3222011904 | bytes 13631488 | tf_op jit(solution)/shard_map/dot_general | solution.py:357
  154.9 1.2 constant_dynamic-slice_fusion
  156.1 0.4 squeeze.4
  156.5 3.3 %convert_element_type.51.parts = bf16[4,192,1024]{2,1,0:T(8,128)(2,1)} convert(f32[4,192,1024]{2,1,0:T(8,128)} %bitcast.79) | non-fusion elementwise | flops 786432 | bytes 4718592 | tf_op jit(solution)/shard_map/convert_element_type | solution.py:361
  159.8 39.3 %shard_map.96 = bf16[4,192,1024]{2,1,0:T(8,128)(2,1)} custom-call(bf16[4,192,1024]{2,1,0:T(8,128)(2,1)} %convert_element_type.51.parts), custom_call_target="tpu_custom_call" | custom-call | tf_op jit(solution)/shard_map/pallas_call | solution.py:306
  199.1 1.9 select_reduce_fusion
  201.0 0.0 copy-start.8
  201.0 0.4 reduce_sum.31
  201.4 0.4 copy_add_fusion
  201.8 0.0 copy-done.8
  201.8 0.1 add_convert_fusion.1
  201.9 0.8 multiply_cosine_fusion
  202.6 0.4 subtract_convert_fusion
  203.0 0.1 slice.51
  203.1 0.4 pad_maximum_fusion
  203.6 0.9 copy.29
  204.5 0.0 copy-done
  204.5 0.0 copy-start.5
  204.5 1.6 fusion.23
  206.0 0.3 copy-done.5
  206.4 1.8 fusion.21
  208.1 0.1 iota_compare_fusion.1
  208.2 1.3 fusion.22
  209.5 0.1 reduce_max.22
  209.6 3.1 %fusion.20 = f32[48,4,4,4]{3,1,2,0:T(4,128)S(1)} fusion(f32[48,4,4,4]{3,1,2,0:T(4,128)S(1)} %reduce_max.22, f32[48,4,4,4,4]{4,3,1,2,0:T(4,128)S(1)} %get-tuple-element.25, f32[48,4,4,4,32]{4,3,1,2,0:T(4,128)S(1)} %get-tuple-element.23), kind=kLoop, calls=%fused_computation.49 | loop fusion | flops 328704 | bytes 466944 | tf_op jit(solution)/shard_map/reduce_sum | solution.py:63
  212.7 2.8 %divide_convert_fusion = bf16[48,4,4,4,36]{4,3,1,2,0:T(4,128)(2,1)S(1)} fusion(f32[48,4,4,4]{3,1,2,0:T(4,128)S(1)} %fusion.20, f32[48,4,4,4]{3,1,2,0:T(4,128)S(1)} %reduce_max.22, f32[48,4,4,4,4]{4,3,1,2,0:T(4,128)S(1)} %get-tuple-element.25, f32[48,4,4,4,32]{4,3,1,2,0:T(4,128)S(1)} %get-tuple-element.23), kind=kLoop, calls=%fused_computation.18 | loop fusion | flops 442368 | bytes 688128 | tf_op jit(solution)/shard_map/convert_element_type | solution.py:63
  215.5 0.6 fusion.2
  216.1 0.9 fusion.5
  216.9 0.5 copy.27
  217.5 1.1 copy.28
  (6 shorter events, 0.0 us)
Async XLA Ops:
  0.6 203.8 %copy-start = (bf16[48,4,16,128]{3,2,1,0:T(8,128)(2,1)S(1)}, bf16[48,4,16,128]{3,2,1,0:T(8,128)(2,1)}, u32[]{:S(2)}) copy-start(bf16[48,4,16,128]{3,2,1,0:T(8,128)(2,1)} %param.9) | copy-start | bytes 2359300
  0.6 2.5 %copy-start.7 = (bf16[16,2,16,4,128]{4,3,2,1,0:T(4,128)(2,1)S(1)}, bf16[16,2,16,4,128]{4,3,2,1,0:T(4,128)(2,1)}, u32[]{:S(2)}) copy-start(bf16[16,2,16,4,128]{4,3,2,1,0:T(4,128)(2,1)} %param.13) | copy-start | bytes 1572868
  0.7 2.6 %copy-start.9 = (s32[48]{0:T(128)S(1)}, s32[48]{0:T(128)}, u32[]{:S(2)}) copy-start(s32[48]{0:T(128)} %param.14) | copy-start | bytes 580
  3.3 2.2 %copy-start.1 = (bf16[16,32,4096]{2,1,0:T(8,128)(2,1)S(1)}, bf16[16,32,4096]{2,1,0:T(8,128)(2,1)}, u32[]{:S(2)}) copy-start(bf16[16,32,4096]{2,1,0:T(8,128)(2,1)} %param.12) | copy-start | bytes 12582916
  111.1 2.7 %copy-start.2 = (bf16[4,192,4096]{2,1,0:T(8,128)(2,1)}, bf16[4,192,4096]{2,1,0:T(8,128)(2,1)S(1)}, u32[]{:S(2)}) copy-start(bf16[4,192,4096]{2,1,0:T(8,128)(2,1)S(1)} %get-tuple-element.10) | copy-start | bytes 18874372
  113.8 1.6 copy-start.3
  145.7 3.4 %copy-start.4 = (bf16[4,192,2048]{2,1,0:T(8,128)(2,1)S(1)}, bf16[4,192,2048]{2,1,0:T(8,128)(2,1)}, u32[]{:S(2)}) copy-start(bf16[4,192,2048]{2,1,0:T(8,128)(2,1)} %copy-done.3) | copy-start | bytes 9437188
  145.7 4.1 %copy-start.6 = (f32[768,1024]{1,0:T(8,128)S(1)}, f32[768,1024]{1,0:T(8,128)}, u32[]{:S(2)}) copy-start(f32[768,1024]{1,0:T(8,128)} %reshape.151) | copy-start | bytes 9437188
  201.0 0.8 copy-start.8
  204.5 1.9 copy-start.5

commit v3 on v2

--- a/solution.py
+++ b/solution.py
@@ -345,23 +345,36 @@
         jnp.where(chosen[:, :, None], projected.reshape(n * count, known, 2 * rank), 0.0), axis=1
     )
     coords = lax.psum(coords, "tp").astype(jnp.bfloat16)
-    spread = jnp.where(chosen[:, :, None], coords[:, None, :], jnp.bfloat16(0))
-    spread = spread.reshape(n * count, known, 2, rank)
-    delta = jnp.einsum(
-        "takr,akrhd->thkd",
-        spread,
-        b_all.reshape(known, 2, rank, heads, pair // 2),
-        preferred_element_type=jnp.float32,
-    )
-    delta = (delta * low_rank_scale).astype(jnp.bfloat16).reshape(n * count, heads * pair)
+    lane = jnp.arange(known * 2 * rank, dtype=jnp.int32)
+    copies = (lane[None, :] % (2 * rank) == jnp.arange(2 * rank, dtype=jnp.int32)[:, None]).astype(
+        jnp.bfloat16
+    )
+    token_names = jnp.broadcast_to(names[:, None], (n * rows_dev, decode_steps)).reshape(n * count)
+    spread = jnp.dot(coords, copies, preferred_element_type=jnp.float32)
+    spread = jnp.where(
+        token_names[:, None] == lane[None, :] // (2 * rank), spread, 0.0
+    ).astype(jnp.bfloat16)
+    depth = pair // 2
+    ups = b_all.reshape(known * 2 * rank, heads * depth)
+    kind = (lane // rank % 2)[:, None]
+    ups = jnp.concatenate(
+        [
+            jnp.where(kind == k, ups[:, h * depth : (h + 1) * depth], jnp.bfloat16(0))
+            for h in range(heads)
+            for k in range(2)
+        ],
+        axis=1,
+    )
+    delta = jnp.dot(spread, ups, preferred_element_type=jnp.float32)
+    delta = (delta * low_rank_scale).astype(jnp.bfloat16)
     partial = jnp.dot(
         slices.reshape(n * count, width), weight, preferred_element_type=jnp.float32
     )
-    partial = (partial + delta.astype(jnp.float32)).reshape(n, count, heads * pair)
-    others = exchange(partial.astype(jnp.bfloat16), n)
-    mine = lax.dynamic_index_in_dim(partial, f, 0, keepdims=False)
+    parts = (partial + delta.astype(jnp.float32)).astype(jnp.bfloat16)
+    parts = parts.reshape(n, count, heads * pair)
+    others = exchange(parts, n)
     slot = jnp.arange(n, dtype=jnp.int32)[:, None, None]
-    summed = mine + jnp.sum(jnp.where(slot == f, 0.0, others.astype(jnp.float32)), axis=0)
+    summed = jnp.sum(jnp.where(slot == f, parts, others).astype(jnp.float32), axis=0)
     summed = summed.reshape(rows_dev, decode_steps, heads, pair)
     positions = (kv_len[:, None] + jnp.arange(decode_steps, dtype=jnp.int32)[None, :]).astype(
         jnp.float32

time: 219 us -> 202 us (0.922)
  local copies, waits for them, and re-layouts: 31.7 us -> 16.9 us
    convert_element_type x2 -> x0, local copies, waits for them, and re-layouts: 11.3 us -> none  [local(): delta.astype(jnp.float32)]
    convert_element_type x1 -> x0, other arithmetic: 3.27 us -> none  [local(): others = exchange(partial.astype(jnp.bfloat16), n)]
    unnamed x24 -> x27, local copies, waits for them, and re-layouts: 13 us -> 11 us
where the time goes in v3:
time: 202 us
  Pallas kernels  145 us (72%)
  matrix products  23.3 us (12%)
  local copies, waits for them, and re-layouts  16.9 us (8%)
  other arithmetic  11.8 us (6%)
  blocking collectives  3.69 us (2%)
    pallas_call x1, Pallas kernels, gather(): pl.pallas_call(functools.partial(gather_kernel, n, m), out_shape=(shape((...  106 us
    pallas_call x1, Pallas kernels, exchange(): pl.pallas_call(functools.partial(exchange_kernel, n), out_shape=jax.Shape...  39.3 us
    dot_general x1, matrix products, local(): lax.dot_general(tok_all.reshape(n * count, half_width), a_all.reshape(kno...  11 us
    unnamed x27, local copies, waits for them, and re-layouts  11 us
    dot_general x1, matrix products, local(): jnp.dot(slices.reshape(n * count, width), weight, preferred_element_type=...  4.57 us

profile of v3, /device:TPU:14, one launch (start us, length us, event | category | flops | bytes accessed | tf_op | source)
XLA Modules:
  0.0 201.7 jit_solution(179737004527578472)
XLA Ops:
  0.6 0.0 copy-start
  0.6 0.0 copy-start.7
  0.7 0.0 copy-start.9
  0.7 2.5 %reshape.219.tok = bf16[192,4096]{1,0:T(8,128)(2,1)S(1)} reshape(bf16[48,4,4096]{2,1,0:T(4,128)(2,1)} %param.8) | data formatting | bytes 3145728 | tf_op jit(solution)/shard_map/reshape | solution.py:326
  3.1 0.0 copy-done.7
  3.1 0.1 copy.84
  3.2 0.0 copy-done.9
  3.3 0.0 copy-start.1
  3.3 2.2 %copy-done.1 = bf16[16,32,4096]{2,1,0:T(8,128)(2,1)S(1)} copy-done((bf16[16,32,4096]{2,1,0:T(8,128)(2,1)S(1)}, bf16[16,32,4096]{2,1,0:T(8,128)(2,1)}, u32[]{:S(2)}) %copy-start.1) | copy-done | bytes 4194328
  5.4 105.7 %shard_map.95 = (bf16[4,192,4096]{2,1,0:T(8,128)(2,1)S(1)}, bf16[4,192,2048]{2,1,0:T(8,128)(2,1)S(1)}, bf16[2,512,4096]{2,1,0:T(8,128)(2,1)}, bf16[2,512,512]{2,1,0:T(8,128)(2,1)S(1)}, s32[4,8,128]{2,1,0:T(8,128)S(1)}) custom-call(bf16[192,4096]{1,0:T(8,128)(2,1)S(1)} %reshape.219.tok, bf16[512,4096]{1,0:T(8,128)(2,1)S(1)} %bitcast.70, ...), custom_call_target="tpu_custom_call" | custom-call | tf_op jit(solution)/shard_map/pallas_call | solution.py:247
  111.1 0.0 copy-start.2
  111.1 2.7 %copy-done.2 = bf16[4,192,4096]{2,1,0:T(8,128)(2,1)} copy-done((bf16[4,192,4096]{2,1,0:T(8,128)(2,1)}, bf16[4,192,4096]{2,1,0:T(8,128)(2,1)S(1)}, u32[]{:S(2)}) %copy-start.2) | copy-done | bytes 6291480
  113.8 0.0 copy-start.3
  113.8 0.2 select_dynamic-update-slice_fusion.7
  114.1 0.3 select_dynamic-update-slice_fusion.6
  114.3 0.3 select_dynamic-update-slice_fusion.5
  114.6 0.3 select_dynamic-update-slice_fusion.4
  114.9 0.3 select_dynamic-update-slice_fusion.3
  115.1 0.3 select_dynamic-update-slice_fusion.2
  115.4 0.3 select_dynamic-update-slice_fusion.1
  115.7 0.3 select_dynamic-update-slice_fusion
  115.9 0.0 copy-done.3
  116.0 0.1 sub.52
  116.0 0.1 iota_compare_fusion.3
  116.1 0.1 broadcast_in_dim.149
  116.2 0.2 copy.37
  116.4 11.0 %select_reduce_fusion = f32[768,32]{0,1:T(8,128)S(1)} fusion(bf16[768,4096,1]{1,0,2:T(8,128)(2,1)} %bitcast.72, bf16[32,32,4096]{2,1,0:T(8,128)(2,1)} %bitcast.81, pred[768,32]{0,1:T(8,128)(4,1)S(1)} %copy.37), kind=kOutput, calls=%fused_computation.4 | convolution fusion | flops 6443999232 | bytes 14802944 | tf_op jit(solution)/shard_map/dot_general | solution.py:338
  127.4 3.7 %psum.7 = bf16[768,32]{0,1:T(8,128)(2,1)S(1)} all-reduce(f32[768,32]{0,1:T(8,128)S(1)} %select_reduce_fusion), channel_id=1, replica_groups=mesh['groups'=2,'fsdp'=4,'rows'=2,'tp'=2] {'tp'}, use_global_device_ids=true, to_apply=%region_1.2 | all-reduce | flops 24576 | bytes 147456 | tf_op jit(solution)/shard_map/psum | solution.py:347
  131.1 0.1 broadcast_in_dim.148
  131.2 0.1 eq.96
  131.3 3.4 %multiply_convert_fusion = bf16[768,1024]{1,0:T(8,128)(2,1)} fusion(bf16[1024,1024]{1,0:T(8,128)(2,1)S(1)} %select_dynamic-update-slice_fusion, s32[1024]{0:T(1024)S(1)} %get-tuple-element.33, s32[768]{0:T(1024)S(1)} %eq.96, s32[1024]{0:T(1024)S(1)} %get-tuple-element.32, bf16[768,32]{0,1:T(8,128)(2,1)S(1)} %psum.7), kind=kOutput, calls=%fused_computation.2 | convolution fusion | flops 1664909312 | bytes 3730432 | tf_op jit(solution)/shard_map/dot_general | solution.py:368
  134.7 0.0 copy-start.10
  134.7 3.4 %copy.56 = bf16[256,8,4,256]{3,1,2,0:T(8,128)(2,1)S(1)} copy(bf16[256,8,4,256]{3,2,1,0:T(4,128)(2,1)} %bitcast.76) | data formatting | bytes 8388608
  138.1 0.0 copy-done.4
  138.1 0.2 copy-done.10
  138.4 4.6 %add_convert_fusion = bf16[768,1024]{1,0:T(8,128)(2,1)} fusion(bf16[768,1024]{1,0:T(8,128)(2,1)S(1)} %copy-done.10, bf16[768,2048]{1,0:T(8,128)(2,1)S(1)} %bitcast.73, bf16[2048,1024]{1,0:T(8,128)(2,1)S(1)} %bitcast.77), kind=kOutput, calls=%fused_computation.1 | convolution fusion | flops 3223584768 | bytes 10485760 | tf_op jit(solution)/shard_map/dot_general | solution.py:370
  142.9 39.3 %shard_map.96 = bf16[4,192,1024]{2,1,0:T(8,128)(2,1)} custom-call(bf16[4,192,1024]{2,1,0:T(8,128)(2,1)} %bitcast.74), custom_call_target="tpu_custom_call" | custom-call | tf_op jit(solution)/shard_map/pallas_call | solution.py:306
  182.2 0.0 copy-done.5
  182.2 2.3 %convert_reduce_fusion = f32[192,1024]{1,0:T(8,128)S(1)} fusion(bf16[4,192,1024]{2,1,0:T(8,128)(2,1)S(1)} %bitcast.75, bf16[4,192,1024]{2,1,0:T(8,128)(2,1)} %shard_map.96, pred[4]{0:T(512)(128)(4,1)S(1)} %iota_compare_fusion.6), kind=kLoop, calls=%fused_computation | loop fusion | flops 2162688 | bytes 3932164 | tf_op jit(solution)/shard_map/reduce_sum | solution.py:377
  184.5 0.0 copy-start.8
  184.5 0.4 reshape.227
  184.9 0.3 fusion.29
  185.2 0.0 copy-done.8
  185.2 0.1 add_convert_fusion.2
  185.2 0.8 multiply_cosine_fusion
  186.0 0.3 subtract_convert_fusion
  186.3 0.1 slice.63
  186.4 0.1 copy.73
  186.5 0.5 pad_maximum_fusion
  186.9 0.9 copy.45
  187.8 0.0 copy-done
  187.8 0.0 copy-start.6
  187.8 1.6 fusion.31
  189.4 0.3 copy-done.6
  189.7 1.8 fusion.28
  191.5 0.1 iota_compare_fusion.4
  191.6 1.3 fusion.30
  192.9 0.1 reduce_max.22
  193.0 2.9 %fusion.27 = f32[48,4,4,4]{3,1,2,0:T(4,128)S(1)} fusion(f32[48,4,4,4]{3,1,2,0:T(4,128)S(1)} %reduce_max.22, f32[48,4,4,4,4]{4,3,1,2,0:T(4,128)S(1)} %get-tuple-element.31, f32[48,4,4,4,32]{4,3,1,2,0:T(4,128)S(1)} %get-tuple-element.29), kind=kLoop, calls=%fused_computation.73 | loop fusion | flops 328704 | bytes 466944 | tf_op jit(solution)/shard_map/reduce_sum | solution.py:63
  195.9 2.8 %divide_convert_fusion = bf16[48,4,4,4,36]{4,3,1,2,0:T(4,128)(2,1)S(1)} fusion(f32[48,4,4,4]{3,1,2,0:T(4,128)S(1)} %fusion.27, f32[48,4,4,4]{3,1,2,0:T(4,128)S(1)} %reduce_max.22, f32[48,4,4,4,4]{4,3,1,2,0:T(4,128)S(1)} %get-tuple-element.31, f32[48,4,4,4,32]{4,3,1,2,0:T(4,128)S(1)} %get-tuple-element.29), kind=kLoop, calls=%fused_computation.15 | loop fusion | flops 442368 | bytes 688128 | tf_op jit(solution)/shard_map/convert_element_type | solution.py:63
  198.7 0.6 fusion.1
  199.2 0.9 fusion.3
  200.1 0.5 copy.43
  200.6 1.1 copy.44
  (11 shorter events, 0.1 us)
Async XLA Ops:
  0.6 187.2 %copy-start = (bf16[48,4,16,128]{3,2,1,0:T(8,128)(2,1)S(1)}, bf16[48,4,16,128]{3,2,1,0:T(8,128)(2,1)}, u32[]{:S(2)}) copy-start(bf16[48,4,16,128]{3,2,1,0:T(8,128)(2,1)} %param.9) | copy-start | bytes 2359300
  0.6 2.5 %copy-start.7 = (bf16[16,2,16,4,128]{4,3,2,1,0:T(4,128)(2,1)S(1)}, bf16[16,2,16,4,128]{4,3,2,1,0:T(4,128)(2,1)}, u32[]{:S(2)}) copy-start(bf16[16,2,16,4,128]{4,3,2,1,0:T(4,128)(2,1)} %param.13) | copy-start | bytes 1572868
  0.7 2.6 %copy-start.9 = (s32[48]{0:T(128)S(1)}, s32[48]{0:T(128)}, u32[]{:S(2)}) copy-start(s32[48]{0:T(128)} %param.14) | copy-start | bytes 580
  3.3 2.2 %copy-start.1 = (bf16[16,32,4096]{2,1,0:T(8,128)(2,1)S(1)}, bf16[16,32,4096]{2,1,0:T(8,128)(2,1)}, u32[]{:S(2)}) copy-start(bf16[16,32,4096]{2,1,0:T(8,128)(2,1)} %param.12) | copy-start | bytes 12582916
  111.1 2.7 %copy-start.2 = (bf16[4,192,4096]{2,1,0:T(8,128)(2,1)}, bf16[4,192,4096]{2,1,0:T(8,128)(2,1)S(1)}, u32[]{:S(2)}) copy-start(bf16[4,192,4096]{2,1,0:T(8,128)(2,1)S(1)} %get-tuple-element.9) | copy-start | bytes 18874372
  113.8 2.1 %copy-start.3 = (bf16[4,192,2048]{2,1,0:T(8,128)(2,1)}, bf16[4,192,2048]{2,1,0:T(8,128)(2,1)S(1)}, u32[]{:S(2)}) copy-start(bf16[4,192,2048]{2,1,0:T(8,128)(2,1)S(1)} %get-tuple-element.7) | copy-start | bytes 9437188
  134.7 3.4 %copy-start.4 = (bf16[4,192,2048]{2,1,0:T(8,128)(2,1)S(1)}, bf16[4,192,2048]{2,1,0:T(8,128)(2,1)}, u32[]{:S(2)}) copy-start(bf16[4,192,2048]{2,1,0:T(8,128)(2,1)} %copy-done.3) | copy-start | bytes 9437188
  134.7 3.6 %copy-start.10 = (bf16[768,1024]{1,0:T(8,128)(2,1)S(1)}, bf16[768,1024]{1,0:T(8,128)(2,1)}, u32[]{:S(2)}) copy-start(bf16[768,1024]{1,0:T(8,128)(2,1)} %multiply_convert_fusion) | copy-start | bytes 4718596
  142.9 39.3 %copy-start.5 = (bf16[768,1024]{1,0:T(8,128)(2,1)S(1)}, bf16[768,1024]{1,0:T(8,128)(2,1)}, u32[]{:S(2)}) copy-start(bf16[768,1024]{1,0:T(8,128)(2,1)} %add_convert_fusion) | copy-start | bytes 4718596
  184.5 0.7 copy-start.8
  187.8 1.9 copy-start.6

commit v4 on v3

--- a/solution.py
+++ b/solution.py
@@ -275,42 +275,13 @@
     )(tok, a, b, ids)
 
 
-def exchange_kernel(n, parts, out, send, recv):
-    f = lax.axis_index("fsdp")
-    barrier = pltpu.get_barrier_semaphore()
+def exchange(parts, f, n):
+    total = lax.dynamic_index_in_dim(parts, f, 0, keepdims=False).astype(jnp.float32)
     for k in range(1, n):
-        pl.semaphore_signal(
-            barrier, inc=1, device_id={"fsdp": lax.rem(f + k, n)}, device_id_type=MESH
-        )
-    pl.semaphore_wait(barrier, n - 1)
-
-    def copy(k):
-        to = lax.rem(f + k, n)
-        return pltpu.make_async_remote_copy(
-            src_ref=parts.at[to],
-            dst_ref=out.at[f],
-            send_sem=send.at[k],
-            recv_sem=recv.at[k],
-            device_id={"fsdp": to},
-            device_id_type=MESH,
-        )
-
-    for k in range(1, n):
-        copy(k).start()
-    for k in range(1, n):
-        copy(k).wait()
-
-
-def exchange(parts, n):
-    anywhere = pl.BlockSpec(memory_space=pl.ANY)
-    return pl.pallas_call(
-        functools.partial(exchange_kernel, n),
-        out_shape=jax.ShapeDtypeStruct(parts.shape, parts.dtype),
-        in_specs=[anywhere],
-        out_specs=anywhere,
-        scratch_shapes=[pltpu.SemaphoreType.DMA((n,)), pltpu.SemaphoreType.DMA((n,))],
-        compiler_params=pltpu.CompilerParams(collective_id=1, has_side_effects=True),
-    )(parts)
+        leaving = lax.dynamic_index_in_dim(parts, lax.rem(f + k, n), 0, keepdims=False)
+        arrived = lax.ppermute(leaving, "fsdp", [(i, (i + k) % n) for i in range(n)])
+        total = total + arrived.astype(jnp.float32)
+    return total
 
 
 def local(tokens, queries, kv_cache, kv_weight, adapter_a, adapter_b, adapter_id, kv_len):
@@ -372,9 +343,7 @@
     )
     parts = (partial + delta.astype(jnp.float32)).astype(jnp.bfloat16)
     parts = parts.reshape(n, count, heads * pair)
-    others = exchange(parts, n)
-    slot = jnp.arange(n, dtype=jnp.int32)[:, None, None]
-    summed = jnp.sum(jnp.where(slot == f, parts, others).astype(jnp.float32), axis=0)
+    summed = exchange(parts, f, n)
     summed = summed.reshape(rows_dev, decode_steps, heads, pair)
     positions = (kv_len[:, None] + jnp.arange(decode_steps, dtype=jnp.int32)[None, :]).astype(
         jnp.float32

time: 202 us -> 205 us (1.015)
  Pallas kernels: 145 us -> 106 us
  waiting for transfers between devices: 0 us -> 24.7 us
  local copies, waits for them, and re-layouts: 16.9 us -> 23 us
  matrix products: 23.3 us -> 29 us
  starting transfers between devices: 0 us -> 5.3 us
    pallas_call x1 -> x0, Pallas kernels: 39.3 us -> none  [exchange(): pl.pallas_call(functools.partial(exchange_kernel, n), out_shape=jax.Shape...]
    ppermute x0 -> x3, waiting for transfers between devices: none -> 24.7 us  [exchange(): lax.ppermute(leaving, 'fsdp', [(i, (i + k) % n) for i in range(n)])]
    ppermute x0 -> x3, starting transfers between devices: none -> 5.3 us  [exchange(): lax.ppermute(leaving, 'fsdp', [(i, (i + k) % n) for i in range(n)])]
    dot_general x1, matrix products: 1.31 us -> 4.41 us  [attend(): jnp.einsum('rsgqd,rpgd->rsgqp', grouped, cache[..., :depth], preferred_el...]
    unnamed x27 -> x31, local copies, waits for them, and re-layouts: 11 us -> 13.9 us
    dot_general x1, matrix products: 4.57 us -> 7.12 us  [local(): jnp.dot(slices.reshape(n * count, width), weight, preferred_element_type=...]
    add x0 -> x1, other arithmetic: none -> 2.36 us  [exchange(): total = total + arrived.astype(jnp.float32)]
    reduce_sum x1 -> x0, other arithmetic: 2.26 us -> none  [local(): jnp.sum(jnp.where(slot == f, parts, others).astype(jnp.float32), axis=0)]
  transfers between devices with their start and end apart: 0 -> 3, of which waited for: 0 -> 2; matrix products, arithmetic and copies ran while one was open for 0% -> 4% of each run, Pallas kernels for 0% -> 0%
where the time goes in v4:
time: 205 us
  Pallas kernels  106 us (52%)
  matrix products  29 us (14%)
  waiting for transfers between devices  24.7 us (12%)
  local copies, waits for them, and re-layouts  23 us (11%)
  other arithmetic  12.6 us (6%)
  starting transfers between devices  5.3 us (3%)
  blocking collectives  3.69 us (2%)
    pallas_call x1, Pallas kernels, gather(): pl.pallas_call(functools.partial(gather_kernel, n, m), out_shape=(shape((...  106 us
    ppermute x3, waiting for transfers between devices, exchange(): lax.ppermute(leaving, 'fsdp', [(i, (i + k) % n) for i in range(n)])  24.7 us
    unnamed x31, local copies, waits for them, and re-layouts  13.9 us
    dot_general x1, matrix products, local(): lax.dot_general(tok_all.reshape(n * count, half_width), a_all.reshape(kno...  11 us
    dot_general x1, matrix products, local(): jnp.dot(slices.reshape(n * count, width), weight, preferred_element_type=...  7.12 us
    ppermute x3, starting transfers between devices, exchange(): lax.ppermute(leaving, 'fsdp', [(i, (i + k) % n) for i in range(n)])  5.3 us
    dot_general x1, matrix products, attend(): jnp.einsum('rsgqd,rpgd->rsgqp', grouped, cache[..., :depth], preferred_el...  4.41 us
  transfers between devices with their start and end apart: 3, of which 2 were waited for; matrix products, arithmetic and copies ran while one was open for 4% of the time, Pallas kernels for 0%

profile of v4, /device:TPU:14, one launch (start us, length us, event | category | flops | bytes accessed | tf_op | source)
XLA Modules:
  0.0 205.1 jit_solution(13791386483346720639)
XLA Ops:
  0.6 0.0 copy-start
  0.6 0.0 copy-start.7
  0.7 0.0 copy-start.12
  0.7 2.4 %reshape.216.tok = bf16[192,4096]{1,0:T(8,128)(2,1)S(1)} reshape(bf16[48,4,4096]{2,1,0:T(4,128)(2,1)} %param.8) | data formatting | bytes 3145728 | tf_op jit(solution)/shard_map/reshape | solution.py:297
  3.2 0.1 copy.84
  3.3 0.0 copy-done.12
  3.3 0.0 copy-start.1
  3.3 2.2 %copy-done.1 = bf16[16,32,4096]{2,1,0:T(8,128)(2,1)S(1)} copy-done((bf16[16,32,4096]{2,1,0:T(8,128)(2,1)S(1)}, bf16[16,32,4096]{2,1,0:T(8,128)(2,1)}, u32[]{:S(2)}) %copy-start.1) | copy-done | bytes 4194328
  5.5 105.7 %shard_map.95 = (bf16[4,192,4096]{2,1,0:T(8,128)(2,1)S(1)}, bf16[4,192,2048]{2,1,0:T(8,128)(2,1)S(1)}, bf16[2,512,4096]{2,1,0:T(8,128)(2,1)}, bf16[2,512,512]{2,1,0:T(8,128)(2,1)S(1)}, s32[4,8,128]{2,1,0:T(8,128)S(1)}) custom-call(bf16[192,4096]{1,0:T(8,128)(2,1)S(1)} %reshape.216.tok, bf16[512,4096]{1,0:T(8,128)(2,1)S(1)} %bitcast.79, ...), custom_call_target="tpu_custom_call" | custom-call | tf_op jit(solution)/shard_map/pallas_call | solution.py:247
  111.2 2.7 %copy-done.2 = bf16[4,192,4096]{2,1,0:T(8,128)(2,1)} copy-done((bf16[4,192,4096]{2,1,0:T(8,128)(2,1)}, bf16[4,192,4096]{2,1,0:T(8,128)(2,1)S(1)}, u32[]{:S(2)}) %copy-start.2) | copy-done | bytes 6291480
  113.9 1.6 copy-done.3
  115.5 0.2 select_dynamic-update-slice_fusion.7
  115.7 0.3 select_dynamic-update-slice_fusion.6
  116.0 0.3 select_dynamic-update-slice_fusion.5
  116.2 0.3 select_dynamic-update-slice_fusion.4
  116.5 0.3 select_dynamic-update-slice_fusion.3
  116.8 0.3 select_dynamic-update-slice_fusion.2
  117.0 0.3 select_dynamic-update-slice_fusion.1
  117.3 0.3 select_dynamic-update-slice_fusion
  117.6 0.1 sub.52
  117.7 0.1 iota_compare_fusion.3
  117.8 0.1 broadcast_in_dim.139
  117.9 0.2 copy.37
  118.0 11.0 %select_reduce_fusion = f32[768,32]{0,1:T(8,128)S(1)} fusion(bf16[768,4096,1]{1,0,2:T(8,128)(2,1)} %bitcast.81, bf16[32,32,4096]{2,1,0:T(8,128)(2,1)} %bitcast.90, pred[768,32]{0,1:T(8,128)(4,1)S(1)} %copy.37), kind=kOutput, calls=%fused_computation.3 | convolution fusion | flops 6443999232 | bytes 14802944 | tf_op jit(solution)/shard_map/dot_general | solution.py:309
  129.0 3.7 %psum.7 = bf16[768,32]{0,1:T(8,128)(2,1)S(1)} all-reduce(f32[768,32]{0,1:T(8,128)S(1)} %select_reduce_fusion), channel_id=1, replica_groups=mesh['groups'=2,'fsdp'=4,'rows'=2,'tp'=2] {'tp'}, use_global_device_ids=true, to_apply=%region_1.2 | all-reduce | flops 24576 | bytes 147456 | tf_op jit(solution)/shard_map/psum | solution.py:318
  132.7 0.1 broadcast_in_dim.138
  132.8 0.1 eq.83
  132.9 5.2 %copy.56 = bf16[256,8,4,256]{3,1,2,0:T(8,128)(2,1)} copy(bf16[256,8,4,256]{3,2,1,0:T(4,128)(2,1)} %bitcast.83) | data formatting | bytes 8388608
  138.1 3.4 %multiply_convert_fusion = bf16[768,1024]{1,0:T(8,128)(2,1)} fusion(bf16[1024,1024]{1,0:T(8,128)(2,1)S(1)} %select_dynamic-update-slice_fusion, s32[1024]{0:T(1024)S(1)} %get-tuple-element.36, s32[768]{0:T(1024)S(1)} %eq.83, s32[1024]{0:T(1024)S(1)} %get-tuple-element.35, bf16[768,32]{0,1:T(8,128)(2,1)S(1)} %psum.7), kind=kOutput, calls=%fused_computation.1 | convolution fusion | flops 1664909312 | bytes 3730432 | tf_op jit(solution)/shard_map/dot_general | solution.py:339
  141.5 7.1 %add_convert_fusion = bf16[768,1024]{1,0:T(8,128)(2,1)S(1)} fusion(bf16[768,1024]{1,0:T(8,128)(2,1)} %multiply_convert_fusion, bf16[768,2048]{1,0:T(8,128)(2,1)} %bitcast.82, bf16[2048,1024]{1,0:T(8,128)(2,1)} %bitcast.84), kind=kOutput, calls=%fused_computation | convolution fusion | flops 3223584768 | bytes 10485760 | tf_op jit(solution)/shard_map/dot_general | solution.py:341
  148.7 0.0 copy-start.11
  148.7 0.9 dynamic-slice_bitcast_fusion.2
  149.6 0.5 collective-permute-start
  150.2 4.8 %collective-permute-start.1 = (bf16[192,1024]{1,0:T(8,128)(2,1)S(1)}, bf16[192,1024]{1,0:T(8,128)(2,1)}, u32[]{:S(2)}, u32[]{:S(2)}) collective-permute-start(bf16[192,1024]{1,0:T(8,128)(2,1)S(1)} %get-tuple-element.24), channel_id=1, source_target_pairs={{0,8},{4,12},{8,0},{12,4},{1,9},{5,13},{9,1},{13,5},{2,10},{6,14},... | collective-permute-start | bytes 1179656 | tf_op jit(solution)/shard_map/ppermute | solution.py:282
  154.9 0.0 collective-permute-start.2
  154.9 0.0 copy-done.11
  155.0 0.1 add_convert_fusion.2
  155.0 0.0 copy-done.6
  155.0 0.1 iota_compare_fusion.4
  155.1 0.0 copy-done.5
  155.1 2.9 %fusion.30 = (bf16[48,32,4,128]{3,2,1,0:T(4,128)(2,1)}, bf16[48,32,4,128]{3,2,1,0:T(4,128)(2,1)S(1)}) fusion(bf16[48,32,4,256]{3,2,1,0:T(4,128)(2,1)S(1)} %copy-done.5), kind=kLoop, calls=%fused_computation.78 | loop fusion | bytes 6291456 | tf_op jit(solution)/shard_map/slice | solution.py:43
  158.0 1.5 multiply_cosine_fusion
  159.5 4.4 %fusion.32 = (f32[48,4,4,4]{3,1,2,0:T(4,128)}, f32[48,4,4,4,32]{4,3,1,2,0:T(4,128)}) fusion(bf16[48,4,4,4,128]{4,3,2,1,0:T(4,128)(2,1)S(1)} %bitcast.69, bf16[48,32,4,128]{3,2,1,0:T(4,128)(2,1)} %get-tuple-element.20, pred[48,32]{1,0:T(8,128)(4,1)S(1)} %iota_compare_fusion.4), kind=kOutput, calls=%fused_computation.80 | convolution fusion | flops 25457664 | bytes 2766336 | tf_op jit(solution)/shard_map/rsgqd,rpgd->rsgqp/dot_general | solution.py:42
  163.9 0.0 collective-permute-done
  163.9 20.7 %collective-permute-done.1 = bf16[192,1024]{1,0:T(8,128)(2,1)} collective-permute-done((bf16[192,1024]{1,0:T(8,128)(2,1)S(1)}, bf16[192,1024]{1,0:T(8,128)(2,1)}, u32[]{:S(2)}, u32[]{:S(2)}) %collective-permute-start.1) | collective-permute-done | bytes 393248 | tf_op jit(solution)/shard_map/ppermute | solution.py:282
  184.5 4.1 %collective-permute-done.2 = bf16[192,1024]{1,0:T(8,128)(2,1)} collective-permute-done((bf16[192,1024]{1,0:T(8,128)(2,1)S(1)}, bf16[192,1024]{1,0:T(8,128)(2,1)}, u32[]{:S(2)}, u32[]{:S(2)}) %collective-permute-start.2) | collective-permute-done | bytes 393248 | tf_op jit(solution)/shard_map/ppermute | solution.py:282
  188.6 2.4 %fusion.7 = f32[192,1024]{1,0:T(8,128)} fusion(bf16[192,1024]{1,0:T(8,128)(2,1)} %collective-permute-done.2, bf16[192,1024]{1,0:T(8,128)(2,1)} %collective-permute-done.1, bf16[192,1024]{1,0:T(8,128)(2,1)S(1)} %collective-permute-done, bf16[4,192,1024]{2,1,0:T(8,128)(2,1)} %bitcast.87, s32[]{:T(128)S(6)} %select_n.148), kind=kLoop, calls=%fused_computation.19 | loop fusion | flops 1376256 | bytes 2359300 | tf_op jit(solution)/shard_map/add | solution.py:283
  191.0 1.5 reshape.224
  192.5 0.3 fusion.31
  192.8 0.1 slice.63
  192.9 0.1 copy.73
  193.0 0.3 subtract_convert_fusion
  193.2 0.4 pad_maximum_fusion
  193.7 0.9 copy.45
  194.6 1.6 fusion.33
  196.2 0.0 copy-done.8
  196.2 0.1 reduce_max.22
  196.3 0.0 copy-done.4
  196.3 2.9 %fusion.29 = f32[48,4,4,4]{3,1,2,0:T(4,128)S(1)} fusion(f32[48,4,4,4]{3,1,2,0:T(4,128)S(1)} %reduce_max.22, f32[48,4,4,4,4]{4,3,1,2,0:T(4,128)S(1)} %get-tuple-element.34, f32[48,4,4,4,32]{4,3,1,2,0:T(4,128)S(1)} %copy-done.4), kind=kLoop, calls=%fused_computation.77 | loop fusion | flops 328704 | bytes 466944 | tf_op jit(solution)/shard_map/reduce_sum | solution.py:63
  199.2 2.8 %divide_convert_fusion = bf16[48,4,4,4,36]{4,3,1,2,0:T(4,128)(2,1)S(1)} fusion(f32[48,4,4,4]{3,1,2,0:T(4,128)S(1)} %fusion.29, f32[48,4,4,4]{3,1,2,0:T(4,128)S(1)} %reduce_max.22, f32[48,4,4,4,4]{4,3,1,2,0:T(4,128)S(1)} %get-tuple-element.34, f32[48,4,4,4,32]{4,3,1,2,0:T(4,128)S(1)} %copy-done.4), kind=kLoop, calls=%fused_computation.14 | loop fusion | flops 442368 | bytes 688128 | tf_op jit(solution)/shard_map/convert_element_type | solution.py:63
  202.0 0.6 fusion.1
  202.6 0.9 fusion.3
  203.5 0.5 copy.43
  204.0 1.1 copy.44
  (20 shorter events, 0.1 us)
Async XLA Ops:
  0.6 158.8 %copy-start = (bf16[48,4,16,128]{3,2,1,0:T(8,128)(2,1)S(1)}, bf16[48,4,16,128]{3,2,1,0:T(8,128)(2,1)}, u32[]{:S(2)}) copy-start(bf16[48,4,16,128]{3,2,1,0:T(8,128)(2,1)} %param.9) | copy-start | bytes 2359300
  0.6 2.5 %copy-start.7 = (bf16[16,2,16,4,128]{4,3,2,1,0:T(4,128)(2,1)S(1)}, bf16[16,2,16,4,128]{4,3,2,1,0:T(4,128)(2,1)}, u32[]{:S(2)}) copy-start(bf16[16,2,16,4,128]{4,3,2,1,0:T(4,128)(2,1)} %param.13) | copy-start | bytes 1572868
  0.7 2.6 %copy-start.12 = (s32[48]{0:T(128)S(1)}, s32[48]{0:T(128)}, u32[]{:S(2)}) copy-start(s32[48]{0:T(128)} %param.14) | copy-start | bytes 580
  3.3 2.2 %copy-start.1 = (bf16[16,32,4096]{2,1,0:T(8,128)(2,1)S(1)}, bf16[16,32,4096]{2,1,0:T(8,128)(2,1)}, u32[]{:S(2)}) copy-start(bf16[16,32,4096]{2,1,0:T(8,128)(2,1)} %param.12) | copy-start | bytes 12582916
  111.2 2.7 %copy-start.2 = (bf16[4,192,4096]{2,1,0:T(8,128)(2,1)}, bf16[4,192,4096]{2,1,0:T(8,128)(2,1)S(1)}, u32[]{:S(2)}) copy-start(bf16[4,192,4096]{2,1,0:T(8,128)(2,1)S(1)} %get-tuple-element.9) | copy-start | bytes 18874372
  113.9 1.6 copy-start.3
  141.5 13.6 %copy-start.5 = (bf16[48,32,4,256]{3,2,1,0:T(4,128)(2,1)S(1)}, bf16[48,32,4,256]{3,2,1,0:T(4,128)(2,1)}, u32[]{:S(2)}) copy-start(bf16[48,32,4,256]{3,2,1,0:T(4,128)(2,1)} %param.10) | copy-start | bytes 9437188
  148.7 6.4 %copy-start.6 = (bf16[768,1024]{1,0:T(8,128)(2,1)}, bf16[768,1024]{1,0:T(8,128)(2,1)S(1)}, u32[]{:S(2)}) copy-start(bf16[768,1024]{1,0:T(8,128)(2,1)S(1)} %add_convert_fusion) | copy-start | bytes 4718596
  148.7 6.3 %copy-start.11 = (s32[48]{0:T(128)S(1)}, s32[48]{0:T(128)}, u32[]{:S(2)}) copy-start(s32[48]{0:T(128)} %param.15) | copy-start | bytes 580
  149.6 14.2 %collective-permute-start = (bf16[192,1024]{1,0:T(8,128)(2,1)}, bf16[192,1024]{1,0:T(8,128)(2,1)S(1)}, u32[]{:S(2)}, u32[]{:S(2)}) collective-permute-start(bf16[192,1024]{1,0:T(8,128)(2,1)} %get-tuple-element.22), channel_id=1, source_target_pairs={{0,4},{4,8},{8,12},{12,0},{1,5},{5,9},{9,13},{13,1},{2,6},{6,10},{... | collective-permute-start | bytes 1179656 | tf_op jit(solution)/shard_map/ppermute | solution.py:282
  150.2 34.4 %collective-permute-start.1 = (bf16[192,1024]{1,0:T(8,128)(2,1)S(1)}, bf16[192,1024]{1,0:T(8,128)(2,1)}, u32[]{:S(2)}, u32[]{:S(2)}) collective-permute-start(bf16[192,1024]{1,0:T(8,128)(2,1)S(1)} %get-tuple-element.24), channel_id=1, source_target_pairs={{0,8},{4,12},{8,0},{12,4},{1,9},{5,13},{9,1},{13,5},{2,10},{6,14},... | collective-permute-start | bytes 1179656 | tf_op jit(solution)/shard_map/ppermute | solution.py:282
  154.9 33.7 %collective-permute-start.2 = (bf16[192,1024]{1,0:T(8,128)(2,1)S(1)}, bf16[192,1024]{1,0:T(8,128)(2,1)}, u32[]{:S(2)}, u32[]{:S(2)}) collective-permute-start(bf16[192,1024]{1,0:T(8,128)(2,1)S(1)} %get-tuple-element.23), channel_id=1, source_target_pairs={{0,12},{4,0},{8,4},{12,8},{1,13},{5,1},{9,5},{13,9},{2,14},{6,2},{... | collective-permute-start | bytes 1179656 | tf_op jit(solution)/shard_map/ppermute | solution.py:282
  191.0 2.0 copy-start.9
  191.0 2.0 copy-start.10
  194.6 1.6 copy-start.8
  194.6 1.7 copy-start.4

commit v5 on v3

--- a/solution.py
+++ b/solution.py
@@ -9,7 +9,7 @@
 from jax.sharding import PartitionSpec as P
 
 ADP_DEV = 16
-CHUNKS = 4
+CHUNKS = 6
 MESH = pl.DeviceIdType.MESH
 
 low_rank_scale = 0.5

time: 202 us -> 202 us (level)
  no operation moved by 1% of the time
where the time goes in v5:
time: 202 us
  Pallas kernels  145 us (72%)
  matrix products  23.3 us (12%)
  local copies, waits for them, and re-layouts  16.9 us (8%)
  other arithmetic  11.8 us (6%)
  blocking collectives  3.69 us (2%)
    pallas_call x1, Pallas kernels, gather(): pl.pallas_call(functools.partial(gather_kernel, n, m), out_shape=(shape((...  106 us
    pallas_call x1, Pallas kernels, exchange(): pl.pallas_call(functools.partial(exchange_kernel, n), out_shape=jax.Shape...  39.1 us
    dot_general x1, matrix products, local(): lax.dot_general(tok_all.reshape(n * count, half_width), a_all.reshape(kno...  11 us
    unnamed x27, local copies, waits for them, and re-layouts  11 us
    dot_general x1, matrix products, local(): jnp.dot(slices.reshape(n * count, width), weight, preferred_element_type=...  4.58 us

profile of v5, /device:TPU:14, one launch (start us, length us, event | category | flops | bytes accessed | tf_op | source)
XLA Modules:
  0.0 202.0 jit_solution(15708743671731405171)
XLA Ops:
  0.6 0.0 copy-start
  0.6 0.0 copy-start.7
  0.7 0.0 copy-start.9
  0.7 2.5 %reshape.219.tok = bf16[192,4096]{1,0:T(8,128)(2,1)S(1)} reshape(bf16[48,4,4096]{2,1,0:T(4,128)(2,1)} %param.8) | data formatting | bytes 3145728 | tf_op jit(solution)/shard_map/reshape | solution.py:326
  3.1 0.0 copy-done.7
  3.1 0.1 copy.84
  3.2 0.0 copy-done.9
  3.3 0.0 copy-start.1
  3.3 2.2 %copy-done.1 = bf16[16,32,4096]{2,1,0:T(8,128)(2,1)S(1)} copy-done((bf16[16,32,4096]{2,1,0:T(8,128)(2,1)S(1)}, bf16[16,32,4096]{2,1,0:T(8,128)(2,1)}, u32[]{:S(2)}) %copy-start.1) | copy-done | bytes 4194328
  5.4 106.1 %shard_map.95 = (bf16[4,192,4096]{2,1,0:T(8,128)(2,1)S(1)}, bf16[4,192,2048]{2,1,0:T(8,128)(2,1)S(1)}, bf16[2,512,4096]{2,1,0:T(8,128)(2,1)}, bf16[2,512,512]{2,1,0:T(8,128)(2,1)S(1)}, s32[4,8,128]{2,1,0:T(8,128)S(1)}) custom-call(bf16[192,4096]{1,0:T(8,128)(2,1)S(1)} %reshape.219.tok, bf16[512,4096]{1,0:T(8,128)(2,1)S(1)} %bitcast.70, ...), custom_call_target="tpu_custom_call" | custom-call | tf_op jit(solution)/shard_map/pallas_call | solution.py:247
  111.5 0.0 copy-start.2
  111.5 2.7 %copy-done.2 = bf16[4,192,4096]{2,1,0:T(8,128)(2,1)} copy-done((bf16[4,192,4096]{2,1,0:T(8,128)(2,1)}, bf16[4,192,4096]{2,1,0:T(8,128)(2,1)S(1)}, u32[]{:S(2)}) %copy-start.2) | copy-done | bytes 6291480
  114.2 0.0 copy-start.3
  114.2 0.2 select_dynamic-update-slice_fusion.7
  114.5 0.3 select_dynamic-update-slice_fusion.6
  114.7 0.3 select_dynamic-update-slice_fusion.5
  115.0 0.3 select_dynamic-update-slice_fusion.4
  115.3 0.3 select_dynamic-update-slice_fusion.3
  115.5 0.3 select_dynamic-update-slice_fusion.2
  115.8 0.3 select_dynamic-update-slice_fusion.1
  116.1 0.3 select_dynamic-update-slice_fusion
  116.3 0.0 copy-done.3
  116.4 0.1 sub.52
  116.4 0.1 iota_compare_fusion.3
  116.5 0.1 broadcast_in_dim.149
  116.6 0.2 copy.37
  116.8 11.0 %select_reduce_fusion = f32[768,32]{0,1:T(8,128)S(1)} fusion(bf16[768,4096,1]{1,0,2:T(8,128)(2,1)} %bitcast.72, bf16[32,32,4096]{2,1,0:T(8,128)(2,1)} %bitcast.81, pred[768,32]{0,1:T(8,128)(4,1)S(1)} %copy.37), kind=kOutput, calls=%fused_computation.4 | convolution fusion | flops 6443999232 | bytes 14802944 | tf_op jit(solution)/shard_map/dot_general | solution.py:338
  127.8 3.7 %psum.7 = bf16[768,32]{0,1:T(8,128)(2,1)S(1)} all-reduce(f32[768,32]{0,1:T(8,128)S(1)} %select_reduce_fusion), channel_id=1, replica_groups=mesh['groups'=2,'fsdp'=4,'rows'=2,'tp'=2] {'tp'}, use_global_device_ids=true, to_apply=%region_1.2 | all-reduce | flops 24576 | bytes 147456 | tf_op jit(solution)/shard_map/psum | solution.py:347
  131.5 0.1 broadcast_in_dim.148
  131.6 0.1 eq.96
  131.7 3.4 %multiply_convert_fusion = bf16[768,1024]{1,0:T(8,128)(2,1)} fusion(bf16[1024,1024]{1,0:T(8,128)(2,1)S(1)} %select_dynamic-update-slice_fusion, s32[1024]{0:T(1024)S(1)} %get-tuple-element.33, s32[768]{0:T(1024)S(1)} %eq.96, s32[1024]{0:T(1024)S(1)} %get-tuple-element.32, bf16[768,32]{0,1:T(8,128)(2,1)S(1)} %psum.7), kind=kOutput, calls=%fused_computation.2 | convolution fusion | flops 1664909312 | bytes 3730432 | tf_op jit(solution)/shard_map/dot_general | solution.py:368
  135.1 0.0 copy-start.4
  135.1 0.0 copy-start.10
  135.2 3.4 %copy.56 = bf16[256,8,4,256]{3,1,2,0:T(8,128)(2,1)S(1)} copy(bf16[256,8,4,256]{3,2,1,0:T(4,128)(2,1)} %bitcast.76) | data formatting | bytes 8388608
  138.5 0.0 copy-done.4
  138.6 0.2 copy-done.10
  138.8 4.6 %add_convert_fusion = bf16[768,1024]{1,0:T(8,128)(2,1)} fusion(bf16[768,1024]{1,0:T(8,128)(2,1)S(1)} %copy-done.10, bf16[768,2048]{1,0:T(8,128)(2,1)S(1)} %bitcast.73, bf16[2048,1024]{1,0:T(8,128)(2,1)S(1)} %bitcast.77), kind=kOutput, calls=%fused_computation.1 | convolution fusion | flops 3223584768 | bytes 10485760 | tf_op jit(solution)/shard_map/dot_general | solution.py:370
  143.3 39.1 %shard_map.96 = bf16[4,192,1024]{2,1,0:T(8,128)(2,1)} custom-call(bf16[4,192,1024]{2,1,0:T(8,128)(2,1)} %bitcast.74), custom_call_target="tpu_custom_call" | custom-call | tf_op jit(solution)/shard_map/pallas_call | solution.py:306
  182.5 0.0 copy-done.5
  182.5 2.3 %convert_reduce_fusion = f32[192,1024]{1,0:T(8,128)S(1)} fusion(bf16[4,192,1024]{2,1,0:T(8,128)(2,1)S(1)} %bitcast.75, bf16[4,192,1024]{2,1,0:T(8,128)(2,1)} %shard_map.96, pred[4]{0:T(512)(128)(4,1)S(1)} %iota_compare_fusion.6), kind=kLoop, calls=%fused_computation | loop fusion | flops 2162688 | bytes 3932164 | tf_op jit(solution)/shard_map/reduce_sum | solution.py:377
  184.8 0.0 copy-start.8
  184.8 0.4 reshape.227
  185.2 0.3 fusion.29
  185.4 0.0 copy-done.8
  185.4 0.1 add_convert_fusion.2
  185.5 0.8 multiply_cosine_fusion
  186.3 0.3 subtract_convert_fusion
  186.6 0.1 slice.63
  186.6 0.1 copy.73
  186.7 0.5 pad_maximum_fusion
  187.2 0.9 copy.45
  188.1 0.0 copy-done
  188.1 1.6 fusion.31
  189.7 0.3 copy-done.6
  190.0 1.8 fusion.28
  191.8 0.1 iota_compare_fusion.4
  191.8 1.3 fusion.30
  193.2 0.1 reduce_max.22
  193.3 2.9 %fusion.27 = f32[48,4,4,4]{3,1,2,0:T(4,128)S(1)} fusion(f32[48,4,4,4]{3,1,2,0:T(4,128)S(1)} %reduce_max.22, f32[48,4,4,4,4]{4,3,1,2,0:T(4,128)S(1)} %get-tuple-element.31, f32[48,4,4,4,32]{4,3,1,2,0:T(4,128)S(1)} %get-tuple-element.29), kind=kLoop, calls=%fused_computation.73 | loop fusion | flops 328704 | bytes 466944 | tf_op jit(solution)/shard_map/reduce_sum | solution.py:63
  196.1 2.8 %divide_convert_fusion = bf16[48,4,4,4,36]{4,3,1,2,0:T(4,128)(2,1)S(1)} fusion(f32[48,4,4,4]{3,1,2,0:T(4,128)S(1)} %fusion.27, f32[48,4,4,4]{3,1,2,0:T(4,128)S(1)} %reduce_max.22, f32[48,4,4,4,4]{4,3,1,2,0:T(4,128)S(1)} %get-tuple-element.31, f32[48,4,4,4,32]{4,3,1,2,0:T(4,128)S(1)} %get-tuple-element.29), kind=kLoop, calls=%fused_computation.15 | loop fusion | flops 442368 | bytes 688128 | tf_op jit(solution)/shard_map/convert_element_type | solution.py:63
  198.9 0.6 fusion.1
  199.5 0.9 fusion.3
  200.4 0.5 copy.43
  200.9 1.1 copy.44
  (11 shorter events, 0.1 us)
Async XLA Ops:
  0.6 187.5 %copy-start = (bf16[48,4,16,128]{3,2,1,0:T(8,128)(2,1)S(1)}, bf16[48,4,16,128]{3,2,1,0:T(8,128)(2,1)}, u32[]{:S(2)}) copy-start(bf16[48,4,16,128]{3,2,1,0:T(8,128)(2,1)} %param.9) | copy-start | bytes 2359300
  0.6 2.5 %copy-start.7 = (bf16[16,2,16,4,128]{4,3,2,1,0:T(4,128)(2,1)S(1)}, bf16[16,2,16,4,128]{4,3,2,1,0:T(4,128)(2,1)}, u32[]{:S(2)}) copy-start(bf16[16,2,16,4,128]{4,3,2,1,0:T(4,128)(2,1)} %param.13) | copy-start | bytes 1572868
  0.7 2.6 %copy-start.9 = (s32[48]{0:T(128)S(1)}, s32[48]{0:T(128)}, u32[]{:S(2)}) copy-start(s32[48]{0:T(128)} %param.14) | copy-start | bytes 580
  3.3 2.2 %copy-start.1 = (bf16[16,32,4096]{2,1,0:T(8,128)(2,1)S(1)}, bf16[16,32,4096]{2,1,0:T(8,128)(2,1)}, u32[]{:S(2)}) copy-start(bf16[16,32,4096]{2,1,0:T(8,128)(2,1)} %param.12) | copy-start | bytes 12582916
  111.5 2.7 %copy-start.2 = (bf16[4,192,4096]{2,1,0:T(8,128)(2,1)}, bf16[4,192,4096]{2,1,0:T(8,128)(2,1)S(1)}, u32[]{:S(2)}) copy-start(bf16[4,192,4096]{2,1,0:T(8,128)(2,1)S(1)} %get-tuple-element.9) | copy-start | bytes 18874372
  114.2 2.1 %copy-start.3 = (bf16[4,192,2048]{2,1,0:T(8,128)(2,1)}, bf16[4,192,2048]{2,1,0:T(8,128)(2,1)S(1)}, u32[]{:S(2)}) copy-start(bf16[4,192,2048]{2,1,0:T(8,128)(2,1)S(1)} %get-tuple-element.7) | copy-start | bytes 9437188
  135.1 3.4 %copy-start.4 = (bf16[4,192,2048]{2,1,0:T(8,128)(2,1)S(1)}, bf16[4,192,2048]{2,1,0:T(8,128)(2,1)}, u32[]{:S(2)}) copy-start(bf16[4,192,2048]{2,1,0:T(8,128)(2,1)} %copy-done.3) | copy-start | bytes 9437188
  135.1 3.6 %copy-start.10 = (bf16[768,1024]{1,0:T(8,128)(2,1)S(1)}, bf16[768,1024]{1,0:T(8,128)(2,1)}, u32[]{:S(2)}) copy-start(bf16[768,1024]{1,0:T(8,128)(2,1)} %multiply_convert_fusion) | copy-start | bytes 4718596
  143.3 39.2 %copy-start.5 = (bf16[768,1024]{1,0:T(8,128)(2,1)S(1)}, bf16[768,1024]{1,0:T(8,128)(2,1)}, u32[]{:S(2)}) copy-start(bf16[768,1024]{1,0:T(8,128)(2,1)} %add_convert_fusion) | copy-start | bytes 4718596
  184.8 0.7 copy-start.8
  188.1 1.9 copy-start.6
